TPU v7x, 512 devices: a whole 4x8x8 slice. The times are simulated.
512 devices in a mesh: dp: 64 (over z, y), expert: 8 (over x, core).
Axes of the slice: x: 4, y: 8, z: 8, core: 2. Of those that a mesh axis runs over, the one named last changes fastest.
Arguments:
- router_grads: float32 [8, 7168, 384], P('expert', 'dp'), may hold values from -120 to 120
- latent_grads: float32 [8, 7168, 576], P('expert', 'dp'), may hold values from -120 to 120
- router_moment: float32 [7168, 384], P('dp'), may hold values from -6 to 6
- latent_moment: float32 [7168, 576], P('dp'), may hold values from -6 to 6
Outputs:
- router_moment_out: float32 [7168, 384], P('dp')
- latent_moment_out: float32 [7168, 576], P('dp')
- router_update: float32 [7168, 384], P('dp')
- latent_update: float32 [7168, 576], P('dp')
All inputs are finite; a program needn't handle non-finite values.
Results may differ from a plain program's by a relative error of at most 0.012.
The roundings to bfloat16 on the way count: a program that leaves them out, or rounds other values in their place, can miss the bound.
Values may be sent and summed in bfloat16 or wider, within the bound.
No kernel may reach another device: no remote copies, remote signals or barrier semaphores. Data moves between devices by JAX's collectives and lax.ppermute only.
A program may use at most 64 MiB of HBM per device.

v0:
```python
import math

import jax
import jax.numpy as jnp
from jax import lax
from jax.sharding import PartitionSpec as P

D = 7168
ITERS = 3


COEF_A = 3.4445
COEF_B = -4.775
COEF_C = 2.0315
BETA = 0.95
EPSILON = 1e-07


def stored(value):
    return lax.optimization_barrier(value.astype(jnp.bfloat16))


def square_dot(left, right):
    return jnp.dot(left, right, preferred_element_type=jnp.float32)


def column_gram(scaled):
    return lax.dot_general(
        scaled, scaled, (((0,), (0,)), ((), ())), preferred_element_type=jnp.float32
    )


def apply_factor(scaled, factor):
    product = lax.dot_general(
        scaled, factor, (((1,), (1,)), ((), ())), preferred_element_type=jnp.float32
    )
    return product * math.sqrt(D)


def whole_chain(gram_low):
    width = gram_low.shape[0]
    identity = jnp.eye(width, dtype=jnp.float32)
    factor = gram_low
    for iteration in range(ITERS):
        if iteration == 0:
            gram_step = gram_low
        else:
            partial_value = stored(square_dot(factor, gram_low))
            gram_step = stored(square_dot(partial_value, factor))
        squared = stored(square_dot(gram_step, gram_step))
        mixture = stored(
            COEF_B * gram_step.astype(jnp.float32) + COEF_C * squared.astype(jnp.float32)
        )
        if iteration == 0:
            factor = stored(COEF_A * identity + mixture.astype(jnp.float32))
        else:
            factor = stored(COEF_A * factor.astype(jnp.float32) + square_dot(mixture, factor))
    return factor


def local(router_grads, latent_grads, router_moment, latent_moment):
    summed = lax.psum((router_grads[0], latent_grads[0]), "expert")
    moments = (router_moment, latent_moment)
    moment_new = tuple((BETA * moments[member] + summed[member] for member in range(2)))
    nesterov = tuple((summed[member] + BETA * moment_new[member] for member in range(2)))
    squares = lax.psum(
        (jnp.sum(nesterov[0] * nesterov[0]), jnp.sum(nesterov[1] * nesterov[1])), "dp"
    )
    scaled = tuple(
        (
            (nesterov[member] / (jnp.sqrt(squares[member]) + EPSILON)).astype(jnp.bfloat16)
            for member in range(2)
        )
    )
    partial_grams = (column_gram(scaled[0]), column_gram(scaled[1]))
    grams = lax.psum((partial_grams[0], partial_grams[1]), "dp")
    grams_low = (stored(grams[0]), stored(grams[1]))
    factors = tuple((whole_chain(grams_low[member]) for member in range(2)))
    router_update = apply_factor(scaled[0], factors[0])
    latent_update = apply_factor(scaled[1], factors[1])
    return (moment_new[0], moment_new[1], router_update, latent_update)


def solution(mesh):
    placed = (P("expert", "dp", None), P("expert", "dp", None), P("dp", None), P("dp", None))
    return jax.shard_map(
        local,
        mesh=mesh,
        in_specs=placed,
        out_specs=(P("dp", None), P("dp", None), P("dp", None), P("dp", None)),
        check_vma=False,
    )
```

profile of v0, /device:TPU:2, one launch (start us, length us, event | category | flops | bytes accessed | tf_op | source)
XLA Modules:
  0.0 552.2 jit_solution(15710468588587470804)
XLA Ops:
  7.2 0.7 all-reduce.6.cloned.1.call-update
  7.9 76.3 %all-reduce.6.cloned.1.call-done = (f32[112,384]{1,0:T(8,128)}, f32[112,576]{1,0:T(8,128)}) async-done(((f32[112,384]{1,0:T(8,128)}, f32[112,576]{1,0:T(8,128)}), (f32[112,384]{1,0:T(8,128)}, f32[112,576]{1,0:T(8,128)})) %all-reduce.6.cloned.1.call-update) | async-done | bytes 430096 | tf_op jit(solution)/shard_map/psum | solution.py:62
  84.2 1.7 multiply_reduce_fusion.1
  85.9 1.8 multiply_reduce_fusion
  87.7 144.9 %all-reduce.1 = (f32[]{:T(128)}, f32[]{:T(128)}) all-reduce(f32[]{:T(128)} %get-tuple-element.12, f32[]{:T(128)} %get-tuple-element.10), channel_id=1, replica_groups=mesh['dp'=64,'expert'=8] {'dp'}, use_global_device_ids=true, to_apply=%region_3.0 | all-reduce | flops 2 | bytes 16 | tf_op jit(solution)/shard_map/psum | solution.py:66
  234.0 0.3 fusion.2
  234.3 0.4 fusion.3
  234.7 296.9 %all-reduce.7 = (bf16[384,384]{1,0:T(8,128)(2,1)S(1)}, bf16[576,576]{1,0:T(8,128)(2,1)}) all-reduce(f32[384,384]{1,0:T(8,128)S(1)} %fusion.2, f32[576,576]{1,0:T(8,128)S(1)} %fusion.3), channel_id=1, replica_groups=mesh['dp'=64,'expert'=8] {'dp'}, use_global_device_ids=true, to_apply=%region_4.0 | all-reduce | flops 479232 | bytes 2875392 | tf_op jit(solution)/shard_map/psum | solution.py:76
  531.6 0.3 convolution_convert_fusion.13
  532.2 0.3 convolution_convert_fusion.12
  532.5 0.3 convolution_convert_fusion.11
  532.8 0.3 convolution_convert_fusion.10
  533.2 0.1 add_convert_fusion.7
  533.3 0.3 fusion
  533.6 0.3 convolution_convert_fusion.9
  534.0 0.3 convolution_convert_fusion.8
  534.3 0.3 convolution_convert_fusion.7
  534.8 0.3 fusion.1
  535.1 0.9 convolution_multiply_fusion.1
  536.1 0.8 convolution_convert_fusion.6
  536.9 0.3 add_convert_fusion.5
  537.3 0.8 convolution_convert_fusion.5
  538.1 0.8 convolution_convert_fusion.4
  538.9 0.8 convolution_convert_fusion.3
  539.7 0.3 add_convert_fusion.3
  539.9 0.8 add_convert_fusion.2
  540.8 0.8 convolution_convert_fusion.2
  541.6 0.8 convolution_convert_fusion.1
  542.4 0.8 convolution_convert_fusion
  543.2 0.3 add_convert_fusion.1
  543.4 0.8 add_convert_fusion
  544.3 1.1 convolution_multiply_fusion
  (17 shorter events, 0.5 us)
Async XLA Ops:
  7.2 77.0 %all-reduce.6.cloned.1.call-start = ((), (), s32[]{:S(2)}) async-start(), calls=%async_computation | async-start | bytes 917504 | tf_op jit(solution)/shard_map/psum | solution.py:62
  84.2 149.7 %copy-start.4 = (f32[112,384]{1,0:T(8,128)S(1)}, f32[112,384]{1,0:T(8,128)}, u32[]{:S(2)}) copy-start(f32[112,384]{1,0:T(8,128)} %get-tuple-element.8) | copy-start | bytes 516100
  84.2 150.1 %copy-start.1 = (f32[112,576]{1,0:T(8,128)S(1)}, f32[112,576]{1,0:T(8,128)}, u32[]{:S(2)}) copy-start(f32[112,576]{1,0:T(8,128)} %get-tuple-element.9) | copy-start | bytes 774148
  85.9 148.8 %copy-start.3 = (f32[112,384]{1,0:T(8,128)}, f32[112,384]{1,0:T(8,128)S(1)}, u32[]{:S(2)}) copy-start(f32[112,384]{1,0:T(8,128)S(1)} %get-tuple-element.13) | copy-start | bytes 516100
  87.7 147.0 %copy-start = (f32[112,576]{1,0:T(8,128)}, f32[112,576]{1,0:T(8,128)S(1)}, u32[]{:S(2)}) copy-start(f32[112,576]{1,0:T(8,128)S(1)} %get-tuple-element.11) | copy-start | bytes 774148
  534.3 1.7 copy-start.2
Sparse Core Ops, SparseCore 0:
  10.5 73.6 all-reduce.5
where the time goes:
time: 552 us
  blocking collectives  442 us (80%)
  waiting for transfers between devices  77 us (14%)
  between operations  15.7 us (3%)
  matrix products  12.8 us (2%)
    psum x1, blocking collectives, local(): grams = lax.psum((partial_grams[0], partial_grams[1]), 'dp')  297 us
    psum x1, blocking collectives, local(): lax.psum((jnp.sum(nesterov[0] * nesterov[0]), jnp.sum(nesterov[1] * neste...  145 us
    psum x1, waiting for transfers between devices, local(): summed = lax.psum((router_grads[0], latent_grads[0]), 'expert')  76.3 us
  transfers between devices with their start and end apart: 1, of which 1 were waited for; matrix products, arithmetic and copies ran while one was open for 0% of the time, Pallas kernels for 0%

commit v1 on v0

v1 whole, which is shorter than its diff:
```python
import math

import jax
import jax.numpy as jnp
from jax import lax
from jax.sharding import Mesh
from jax.sharding import PartitionSpec as P

D = 7168
ITERS = 3
R = 384
L = 576
T = 128

COEF_A = 3.4445
COEF_B = -4.775
COEF_C = 2.0315
BETA = 0.95
EPSILON = 1e-07
BF = jnp.bfloat16
F32 = jnp.float32


def stored(value):
    return lax.optimization_barrier(value.astype(BF))


def square_dot(left, right):
    return jnp.dot(left, right, preferred_element_type=F32)


def column_gram(value):
    return lax.dot_general(value, value, (((0,), (0,)), ((), ())), preferred_element_type=F32)


def apply_factor(scaled, factor):
    product = lax.dot_general(
        scaled, factor, (((1,), (1,)), ((), ())), preferred_element_type=F32
    )
    return product * math.sqrt(D)


def whole_chain(gram_low):
    width = gram_low.shape[0]
    identity = jnp.eye(width, dtype=F32)
    factor = gram_low
    for iteration in range(ITERS):
        if iteration == 0:
            gram_step = gram_low
        else:
            partial_value = stored(square_dot(factor, gram_low))
            gram_step = stored(square_dot(partial_value, factor))
        squared = stored(square_dot(gram_step, gram_step))
        mixture = stored(COEF_B * gram_step.astype(F32) + COEF_C * squared.astype(F32))
        if iteration == 0:
            factor = stored(COEF_A * identity + mixture.astype(F32))
        else:
            factor = stored(COEF_A * factor.astype(F32) + square_dot(mixture, factor))
    return factor


def split3(value):
    high = lax.reduce_precision(value, 8, 7)
    rest = value - high
    middle = lax.reduce_precision(rest, 8, 7)
    return [high, middle, rest - middle]


def pack(gram_r, gram_l):
    tiles = [
        gram_r[T * i : T * (i + 1), T * j : T * (j + 1)] for i in range(3) for j in range(i, 3)
    ]
    tiles += [
        gram_l[T * i : T * (i + 1), T * j : T * (j + 1)] for i in range(4) for j in range(i, 4)
    ]
    tiles += [gram_l[512:576, T * j : T * (j + 1)] for j in range(4)]
    corner = gram_l[512:576, 512:576]
    tiles.append(jnp.concatenate([corner, jnp.zeros_like(corner)], axis=1))
    tiles.append(jnp.zeros((64, T), corner.dtype))
    return jnp.concatenate(tiles, axis=0)


def unpack(packed):
    at = 0
    whole = []
    for blocks in (3, 4):
        tile = {}
        for i in range(blocks):
            for j in range(i, blocks):
                tile[i, j] = packed[T * at : T * (at + 1)]
                if i != j:
                    tile[j, i] = tile[i, j].T
                at += 1
        whole.append(
            jnp.concatenate(
                [
                    jnp.concatenate([tile[i, j] for j in range(blocks)], axis=1)
                    for i in range(blocks)
                ],
                axis=0,
            )
        )
    base = T * at
    strip = jnp.concatenate([packed[base + 64 * j : base + 64 * (j + 1)] for j in range(4)], axis=1)
    corner = packed[base + 256 : base + 320, :64]
    top = jnp.concatenate([whole[1], strip.T], axis=1)
    bottom = jnp.concatenate([strip, corner], axis=1)
    return whole[0], jnp.concatenate([top, bottom], axis=0)


def local(router_grads, latent_grads, router_moment, latent_moment):
    swap = [(0, 1), (1, 0)]
    router, latent = router_grads[0], latent_grads[0]
    router = router + lax.ppermute(router, "core", swap)
    latent = latent + lax.ppermute(latent, "core", swap)
    chip = stored(jnp.concatenate([router, latent], axis=1))
    parts = lax.all_to_all(jnp.broadcast_to(chip[None], (4,) + chip.shape), "x", 0, 0)
    parts = parts.astype(F32)
    summed = (parts[0] + parts[1]) + (parts[2] + parts[3])

    moments = (router_moment, latent_moment)
    sums = (summed[:, :R], summed[:, R:])
    moment_new = tuple(BETA * moments[k] + sums[k] for k in range(2))
    nesterov = tuple(sums[k] + BETA * moment_new[k] for k in range(2))
    squares = [jnp.sum(nesterov[k] * nesterov[k]) for k in range(2)]
    grams = [column_gram(nesterov[k].astype(BF)) for k in range(2)]
    extra = jnp.stack(split3(squares[0]) + split3(squares[1]))
    extra = jnp.pad(extra, (0, T - 6))
    extra = jnp.broadcast_to(extra[None, None], (64, 2, T))
    packed = pack(grams[0], grams[1]).reshape(64, 38, T)
    payload = stored(jnp.concatenate([packed, extra], axis=1))
    pieces = lax.all_to_all(payload, "dp", 0, 0).astype(F32)
    piece = jnp.sum(pieces, axis=0)
    totals = piece[38]
    squares = [totals[0] + totals[1] + totals[2], totals[3] + totals[4] + totals[5]]
    magnitudes = [jnp.sqrt(square) + EPSILON for square in squares]
    inverse = [1.0 / (magnitude * magnitude) for magnitude in magnitudes]
    row = lax.axis_index("dp") * 38 + lax.iota(jnp.int32, 38)
    scale = jnp.where(row < 6 * T, inverse[0], inverse[1])
    low = stored(piece[:38] * scale[:, None])
    low = jnp.pad(low, ((0, 2), (0, 0)))
    low = lax.all_to_all(jnp.broadcast_to(low[None], (64,) + low.shape), "dp", 0, 0)
    grams_low = unpack(low[:, :38].reshape(19 * T, T))
    updates = []
    for k in range(2):
        scaled = (nesterov[k] / magnitudes[k]).astype(BF)
        updates.append(apply_factor(scaled, whole_chain(stored(grams_low[k]))))
    return (moment_new[0], moment_new[1], updates[0], updates[1])


def solution(mesh):
    inner = Mesh(mesh.devices.reshape(64, 4, 2), ("dp", "x", "core"))
    group = ("x", "core")
    return jax.shard_map(
        local,
        mesh=inner,
        in_specs=(P(group, "dp", None), P(group, "dp", None), P("dp", None), P("dp", None)),
        out_specs=(P("dp", None),) * 4,
        check_vma=False,
    )
```

time: 552 us -> 126 us (0.23)
  the two profiles are of different devices: /device:TPU:2 before, /device:TPU:8 now
where the time goes in v1:
time: 126 us; the launch traced here: 125 us
  blocking collectives  44.7 us (35%)
  waiting for transfers between devices  21.9 us (17%)
  starting transfers between devices  20.9 us (17%)
  matrix products  12.9 us (10%)
  between operations  12.2 us (10%)
  local copies, waits for them, and re-layouts  6.55 us (5%)
  other arithmetic  6.25 us (5%)
    all_to_all x1, blocking collectives, local(): lax.all_to_all(jnp.broadcast_to(low[None], (64,) + low.shape), 'dp', 0, 0)  26.4 us
    all_to_all x1, waiting for transfers between devices, local(): pieces = lax.all_to_all(payload, 'dp', 0, 0).astype(F32)  21.5 us
    all_to_all x1, blocking collectives, local(): lax.all_to_all(jnp.broadcast_to(chip[None], (4,) + chip.shape), 'x', 0, 0)  18.3 us
    all_to_all x1, starting transfers between devices, local(): pieces = lax.all_to_all(payload, 'dp', 0, 0).astype(F32)  16.6 us
    dot_general x18, matrix products, square_dot(): return jnp.dot(left, right, preferred_element_type=F32)  10.2 us
  transfers between devices with their start and end apart: 3, of which 2 were waited for; matrix products, arithmetic and copies ran while one was open for 1% of the time, Pallas kernels for 0%

profile of v1, /device:TPU:8, one launch (start us, length us, event | category | flops | bytes accessed | tf_op | source)
XLA Modules:
  0.0 125.5 jit_solution(6193223812544944197)
XLA Ops:
  0.6 1.9 %collective-permute-start = (f32[112,384]{1,0:T(8,128)}, f32[112,384]{1,0:T(8,128)S(1)}, u32[]{:S(2)}, u32[]{:S(2)}) collective-permute-start(f32[112,384]{1,0:T(8,128)} %bitcast.76), channel_id=1, source_target_pairs={{0,1},{1,0},{2,3},{3,2},{4,5},{5,4},{6,7},{7,6},{8,9},{9,8},{10,11... | collective-permute-start | bytes 516104 | tf_op jit(solution)/shard_map/ppermute | solution.py:114
  2.6 2.4 %collective-permute-start.1 = (f32[112,576]{1,0:T(8,128)}, f32[112,576]{1,0:T(8,128)S(1)}, u32[]{:S(2)}, u32[]{:S(2)}) collective-permute-start(f32[112,576]{1,0:T(8,128)} %bitcast.75), channel_id=1, source_target_pairs={{0,1},{1,0},{2,3},{3,2},{4,5},{5,4},{6,7},{7,6},{8,9},{9,8},{10,11... | collective-permute-start | bytes 774152 | tf_op jit(solution)/shard_map/ppermute | solution.py:115
  5.0 0.9 add_convert_fusion.11
  5.9 0.4 collective-permute-done.1
  6.4 1.0 add_convert_fusion.10
  7.5 18.3 %all_to_all.15 = bf16[4,112,960]{2,1,0:T(8,128)(2,1)S(1)} all-to-all(bf16[4,112,960]{2,1,0:T(8,128)(2,1)S(1)} %broadcast_in_dim.16), channel_id=1, replica_groups=mesh['dp'=64,'x'=4,'core'=2] {'x'}, dimensions={0} | all-to-all | bytes 1720320 | tf_op jit(solution)/shard_map/all_to_all | solution.py:117
  26.2 0.8 copy-done.3
  27.0 0.6 multiply_reduce_fusion.1
  31.1 0.7 multiply_reduce_fusion
  35.3 2.5 %stack.27 = bf16[6]{0:T(256)(128)(2,1)S(1)} concatenate(f32[1]{0:T(128)} %bitcast.3, f32[1]{0:T(128)} %bitcast.4, bf16[1]{0:T(256)(128)(2,1)} %bitcast.5, f32[1]{0:T(128)} %bitcast.6, f32[1]{0:T(128)} %bitcast.7, bf16[1]{0:T(256)(128)(2,1)} %bitcast.8), dimensions={0} | concatenate | bytes 32 | tf_op jit(solution)/shard_map/stack | solution.py:127
  38.2 0.4 convolution_convert_fusion.7
  39.1 0.9 pad_maximum_fusion.1
  40.0 16.6 %all-to-all-start.1 = ((bf16[64,40,128]{2,1,0:T(8,128)(2,1)}), bf16[64,40,128]{2,1,0:T(8,128)(2,1)S(1)}, u32[]{:S(2)}, u32[]{:S(2)}) async-start(bf16[64,40,128]{2,1,0:T(8,128)(2,1)} %pad_maximum_fusion.1), calls=%async_computation.1 | async-start | bytes 1310720 | tf_op jit(solution)/shard_map/all_to_all | solution.py:132
  56.6 21.5 %all-to-all-done.1 = bf16[64,40,128]{2,1,0:T(8,128)(2,1)S(1)} async-done(((bf16[64,40,128]{2,1,0:T(8,128)(2,1)}), bf16[64,40,128]{2,1,0:T(8,128)(2,1)S(1)}, u32[]{:S(2)}, u32[]{:S(2)}) %all-to-all-start.1) | async-done | bytes 655392 | tf_op jit(solution)/shard_map/all_to_all | solution.py:132
  78.2 0.7 fusion.12
  83.0 26.4 %all_to_all.16 = bf16[64,40,128]{2,1,0:T(8,128)(2,1)S(1)} all-to-all(bf16[64,40,128]{2,1,0:T(8,128)(2,1)S(1)} %broadcast_in_dim.36), channel_id=1, replica_groups=mesh['dp'=64,'x'=4,'core'=2] {'dp'}, dimensions={0} | all-to-all | bytes 1310720 | tf_op jit(solution)/shard_map/all_to_all | solution.py:142
  112.2 0.3 convolution_convert_fusion.13
  112.6 0.3 convolution_convert_fusion.12
  113.4 0.3 fusion
  113.7 0.3 convolution_convert_fusion.10
  114.8 0.3 fusion.1
  115.2 0.9 convolution_multiply_fusion.1
  116.1 0.8 convolution_convert_fusion.6
  117.3 0.8 convolution_convert_fusion.5
  118.1 0.8 convolution_convert_fusion.4
  118.9 0.8 convolution_convert_fusion.3
  120.0 0.8 add_convert_fusion.2
  120.8 0.8 convolution_convert_fusion.2
  121.6 0.8 convolution_convert_fusion.1
  122.5 0.8 convolution_convert_fusion
  123.5 0.8 add_convert_fusion
  124.4 1.1 convolution_multiply_fusion
  (82 shorter events, 6.3 us)
Async XLA Ops:
  0.6 4.3 %collective-permute-start = (f32[112,384]{1,0:T(8,128)}, f32[112,384]{1,0:T(8,128)S(1)}, u32[]{:S(2)}, u32[]{:S(2)}) collective-permute-start(f32[112,384]{1,0:T(8,128)} %bitcast.76), channel_id=1, source_target_pairs={{0,1},{1,0},{2,3},{3,2},{4,5},{5,4},{6,7},{7,6},{8,9},{9,8},{10,11... | collective-permute-start | bytes 516104 | tf_op jit(solution)/shard_map/ppermute | solution.py:114
  2.6 3.8 %collective-permute-start.1 = (f32[112,576]{1,0:T(8,128)}, f32[112,576]{1,0:T(8,128)S(1)}, u32[]{:S(2)}, u32[]{:S(2)}) collective-permute-start(f32[112,576]{1,0:T(8,128)} %bitcast.75), channel_id=1, source_target_pairs={{0,1},{1,0},{2,3},{3,2},{4,5},{5,4},{6,7},{7,6},{8,9},{9,8},{10,11... | collective-permute-start | bytes 774152 | tf_op jit(solution)/shard_map/ppermute | solution.py:115
  26.0 0.9 copy-start.3
  26.0 5.1 %copy-start.2 = (f32[112,576]{1,0:T(8,128)S(1)}, f32[112,576]{1,0:T(8,128)}, u32[]{:S(2)}) copy-start(f32[112,576]{1,0:T(8,128)} %param.7) | copy-start | bytes 774148
  27.6 87.6 %copy-start.1 = (f32[112,384]{1,0:T(8,128)}, f32[112,384]{1,0:T(8,128)S(1)}, u32[]{:S(2)}) copy-start(f32[112,384]{1,0:T(8,128)S(1)} %get-tuple-element.7) | copy-start | bytes 516100
  31.8 92.5 %copy-start = (f32[112,576]{1,0:T(8,128)}, f32[112,576]{1,0:T(8,128)S(1)}, u32[]{:S(2)}) copy-start(f32[112,576]{1,0:T(8,128)S(1)} %get-tuple-element.5) | copy-start | bytes 774148
  40.0 38.1 %all-to-all-start.1 = ((bf16[64,40,128]{2,1,0:T(8,128)(2,1)}), bf16[64,40,128]{2,1,0:T(8,128)(2,1)S(1)}, u32[]{:S(2)}, u32[]{:S(2)}) async-start(bf16[64,40,128]{2,1,0:T(8,128)(2,1)} %pad_maximum_fusion.1), calls=%async_computation.1 | async-start | bytes 1310720 | tf_op jit(solution)/shard_map/all_to_all | solution.py:132

commit v2 on v0

v2 whole, which is shorter than its diff:
```python
import functools
import math

import jax
import jax.numpy as jnp
from jax import lax
from jax.experimental import pallas as pl
from jax.experimental.pallas import tpu as pltpu
from jax.sharding import Mesh
from jax.sharding import PartitionSpec as P

D = 7168
ITERS = 3
ROWS = 112
R = 384
L = 576
LP = 640
T = 128
DP = 64
SLABS = 15
PIECE = 16

COEF_A = 3.4445
COEF_B = -4.775
COEF_C = 2.0315
BETA = 0.95
EPSILON = 1e-07
BF = jnp.bfloat16
F32 = jnp.float32

VMEM = pl.BlockSpec(memory_space=pltpu.VMEM)
PARAMS = pltpu.CompilerParams(vmem_limit_bytes=48 * 1024 * 1024)


def dot(left, right):
    return jnp.dot(left, right, preferred_element_type=F32)


def iota(shape, dim):
    return lax.broadcasted_iota(jnp.int32, shape, dim)


def chip_sum_kernel(router, router_other, latent, latent_other, out):
    a = (router[...] + router_other[...]).astype(BF)
    b = (latent[...] + latent_other[...]).astype(BF)
    for copy in range(4):
        out[copy, :, :R] = a
        out[copy, :, R:] = b


def split3(value):
    high = value.astype(BF).astype(F32)
    rest = value - high
    middle = rest.astype(BF).astype(F32)
    return high, middle, rest - middle


def gram_kernel(parts, moment_r, moment_l, new_r, new_l, nest_r, nest_l, payload, slabs, wide):
    core = lax.axis_index("core")
    squares = []
    grams = []
    for first, width, moment, new, nest in (
        (0, R, moment_r, new_r, nest_r),
        (R, L, moment_l, new_l, nest_l),
    ):
        part = [parts[k, :, first : first + width].astype(F32) for k in range(4)]
        summed = (part[0] + part[1]) + (part[2] + part[3])
        fresh = BETA * moment[...] + summed
        nesterov = summed + BETA * fresh
        new[...] = fresh
        nest[...] = nesterov
        squares.append(jnp.sum(nesterov * nesterov))
        low = nesterov.astype(BF)
        if width == L:
            low = jnp.concatenate([low, jnp.zeros((ROWS, LP - L), BF)], axis=1)
        gram = lax.dot_general(low, low, (((0,), (0,)), ((), ())), preferred_element_type=F32)
        grams.append(gram)

    def tile(k, i, j):
        return grams[k][T * i : T * (i + 1), T * j : T * (j + 1)]

    row, lane = iota((T, T), 0), iota((T, T), 1)

    def fold(upper, lower):
        return jnp.where(row <= lane, upper, lower)

    half = iota((64, T), 1) < 64
    last = tile(0, 2, 2)
    corner = jnp.where(half, tile(1, 4, 4)[:64], last[64:])
    tiles = [
        tile(0, 0, 1),
        tile(0, 0, 2),
        tile(0, 1, 2),
        fold(tile(0, 0, 0), tile(0, 1, 1)),
        jnp.concatenate([last[:64], corner], axis=0),
        tile(1, 0, 1),
        tile(1, 0, 2),
        tile(1, 0, 3),
        tile(1, 1, 2),
        tile(1, 1, 3),
        tile(1, 2, 3),
        fold(tile(1, 0, 0), tile(1, 1, 1)),
        fold(tile(1, 2, 2), tile(1, 3, 3)),
    ]
    pieces = [t[64 * h : 64 * (h + 1)] for t in tiles for h in range(2)]
    pieces += [grams[1][512:576, T * j : T * (j + 1)] for j in range(4)]

    parts6 = split3(squares[0]) + split3(squares[1])
    lane1 = iota((64, T), 1)
    row1 = iota((64, T), 0)
    extra = jnp.zeros((64, T), F32)
    for k in range(6):
        extra = jnp.where(lane1 == k, parts6[k], extra)
    for k, (which, i) in enumerate(((0, 1), (1, 1), (1, 3))):
        diagonal = jnp.sum(jnp.where(row == lane, tile(which, i, i), 0.0), axis=0, keepdims=True)
        low_half = pltpu.roll(diagonal, 64, 1)
        extra = jnp.where((row1 == 2 * k) & (lane1 >= 64), low_half, extra)
        extra = jnp.where((row1 == 2 * k + 1) & (lane1 >= 64), diagonal, extra)

    for c in range(2):

        @pl.when(core == c)
        def _():
            for s in range(SLABS):
                slabs[pl.ds(s, DP, stride=PIECE), :] = pieces[SLABS * c + s]

    slabs[pl.ds(SLABS, DP, stride=PIECE), :] = extra
    payload[...] = slabs[...].astype(BF)


def scale_kernel(pieces, low, magnitude):
    core, here = lax.axis_index("core"), lax.axis_index("dp")
    total = jnp.sum(pieces[...].reshape(DP, PIECE, T).astype(F32), axis=0)
    last = total[SLABS : SLABS + 1]
    lane1 = iota((1, T), 1)
    router = jnp.sum(jnp.where(lane1 < 3, last, 0.0), axis=1, keepdims=True)
    latent = jnp.sum(jnp.where((lane1 >= 3) & (lane1 < 6), last, 0.0), axis=1, keepdims=True)
    router = jnp.sqrt(router) + EPSILON
    latent = jnp.sqrt(latent) + EPSILON
    inverse_r = 1.0 / (router * router)
    inverse_l = 1.0 / (latent * latent)
    row, lane = iota((PIECE, T), 0), iota((PIECE, T), 1)
    slab = SLABS * core + row
    of_router = (slab < 9) | ((slab == 9) & (lane >= 64))
    of_router = jnp.where(row == SLABS, jnp.where(here < 2, 1, 0), jnp.where(of_router, 1, 0))
    scaled = (total * jnp.where(of_router == 1, inverse_r, inverse_l)).astype(BF)
    for k in range(DP):
        low[PIECE * k : PIECE * (k + 1), :] = scaled
    magnitude[...] = jnp.where(iota((8, T), 0) == 0, router, latent)


def update_kernel(
    mine, other, magnitude, nest_r, nest_l, out_r, out_l,
    halves, gram_r, gram_l, step_r, step_l, mix_r, mix_l, fac_r, fac_l, tmp_r, tmp_l,
):
    core = lax.axis_index("core")
    a, b = mine[...].astype(F32), other[...].astype(F32)
    first = core == 0
    halves[0] = jnp.where(first, a, b)
    halves[1] = jnp.where(first, b, a)

    def slab(g):
        return halves[g // SLABS, pl.ds(g % SLABS, DP, stride=PIECE), :]

    def tile(t):
        return jnp.concatenate([slab(2 * t), slab(2 * t + 1)], axis=0)

    def put(ref, i, j, value):
        ref[T * i : T * (i + 1), T * j : T * (j + 1)] = value.astype(BF)

    extra = halves[0, pl.ds(SLABS, 8, stride=PIECE), :]
    row, lane = iota((T, T), 0), iota((T, T), 1)
    lane1 = iota((1, T), 1)

    def both(ref, i, j, value):
        put(ref, i, j, value)
        put(ref, j, i, value.T)

    def unfold(ref, i, j, value, k):
        flipped = value.T
        put(ref, i, i, jnp.where(row <= lane, value, flipped))
        low_half = pltpu.roll(extra[2 * k : 2 * k + 1], 64, 1)
        diagonal = jnp.where(lane1 < 64, low_half, extra[2 * k + 1 : 2 * k + 2])
        inner = jnp.where(row > lane, value, flipped)
        put(ref, j, j, jnp.where(row == lane, diagonal, inner))

    both(gram_r, 0, 1, tile(0))
    both(gram_r, 0, 2, tile(1))
    both(gram_r, 1, 2, tile(2))
    unfold(gram_r, 0, 1, tile(3), 0)
    last = tile(4)
    put(gram_r, 2, 2, jnp.where(row <= lane, last, last.T))
    gram_l[L:, :] = jnp.zeros((LP - L, LP), BF)
    gram_l[512:L, 512:] = jnp.where(iota((64, T), 1) < 64, last[64:], 0.0).astype(BF)
    both(gram_l, 0, 1, tile(5))
    both(gram_l, 0, 2, tile(6))
    both(gram_l, 0, 3, tile(7))
    both(gram_l, 1, 2, tile(8))
    both(gram_l, 1, 3, tile(9))
    both(gram_l, 2, 3, tile(10))
    unfold(gram_l, 0, 1, tile(11), 1)
    unfold(gram_l, 2, 3, tile(12), 2)
    for j in range(4):
        strip = jnp.concatenate([slab(26 + j), jnp.zeros((64, T), F32)], axis=0)
        gram_l[512:L, T * j : T * (j + 1)] = strip[:64].astype(BF)
        put(gram_l, j, 4, strip.T)

    for ref in (step_l, mix_l, fac_l, tmp_l):
        ref[L:, :] = jnp.zeros((LP - L, LP), BF)

    def product(left, right, rows, width, epilogue):
        for start in range(0, width, 256):
            stop = min(start + 256, width)
            acc = dot(left[:rows, :], right[:, start:stop])
            epilogue(acc, start, stop)

    def chain(gram, step, mix, fac, tmp, rows, width):
        def store(ref):
            def epilogue(acc, start, stop):
                ref[:rows, start:stop] = acc.astype(BF)

            return epilogue

        for iteration in range(ITERS):
            if iteration == 0:
                now = gram
            else:
                now = step
                product(fac, gram, rows, width, store(tmp))
                yield
                product(tmp, fac, rows, width, store(step))
                yield

            def mixing(acc, start, stop, now=now):
                squared = acc.astype(BF).astype(F32)
                value = COEF_B * now[:rows, start:stop].astype(F32) + COEF_C * squared
                value = value.astype(BF)
                mix[:rows, start:stop] = value
                if iteration == 0:
                    shape = (rows, stop - start)
                    eye = (iota(shape, 0) == iota(shape, 1) + start).astype(F32)
                    fac[:rows, start:stop] = (COEF_A * eye + value.astype(F32)).astype(BF)

            product(now, now, rows, width, mixing)
            yield
            if iteration > 0:

                def blend(acc, start, stop):
                    value = COEF_A * fac[:rows, start:stop].astype(F32) + acc
                    tmp[:rows, start:stop] = value.astype(BF)

                product(mix, fac, rows, width, blend)
                fac, tmp = tmp, fac
                yield
        yield fac

    chains = (
        chain(gram_r, step_r, mix_r, fac_r, tmp_r, R, R),
        chain(gram_l, step_l, mix_l, fac_l, tmp_l, L, LP),
    )
    factors = [None, None]
    for _ in range(4 * ITERS - 2):
        factors = [next(c) for c in chains]
    root = math.sqrt(D)
    contract = (((1,), (1,)), ((), ()))
    scaled = (nest_r[...] / magnitude[0:1, 0:1]).astype(BF)
    out_r[...] = lax.dot_general(scaled, factors[0][...], contract, preferred_element_type=F32) * root
    scaled = (nest_l[...] / magnitude[1:2, 0:1]).astype(BF)
    scaled = jnp.concatenate([scaled, jnp.zeros((ROWS, LP - L), BF)], axis=1)
    out_l[...] = (
        lax.dot_general(scaled, factors[1][:L, :], contract, preferred_element_type=F32) * root
    )


def call(kernel, out_shape, scratch, name, *args):
    return pl.pallas_call(
        kernel,
        out_shape=out_shape,
        in_specs=[VMEM] * len(args),
        out_specs=jax.tree.map(lambda _: VMEM, out_shape),
        scratch_shapes=scratch,
        compiler_params=PARAMS,
        name=name,
    )(*args)


def local(router_grads, latent_grads, router_moment, latent_moment):
    shape = jax.ShapeDtypeStruct
    swap = [(0, 1), (1, 0)]
    router, latent = router_grads[0], latent_grads[0]
    router_other = lax.ppermute(router, "core", swap)
    latent_other = lax.ppermute(latent, "core", swap)
    chip = call(
        chip_sum_kernel, shape((4, ROWS, R + L), BF), [], "chip_sum",
        router, router_other, latent, latent_other,
    )
    parts = lax.all_to_all(chip, "x", 0, 0)
    new_r, new_l, nest_r, nest_l, payload = call(
        gram_kernel,
        (
            shape((ROWS, R), F32), shape((ROWS, L), F32),
            shape((ROWS, R), F32), shape((ROWS, L), F32),
            shape((DP * PIECE, T), BF),
        ),
        [pltpu.VMEM((DP * PIECE, T), F32), pltpu.VMEM((ROWS, LP), BF)],
        "momentum_gram", parts, router_moment, latent_moment,
    )
    pieces = lax.all_to_all(payload.reshape(DP, PIECE, T), "dp", 0, 0)
    low, magnitude = call(
        scale_kernel,
        (shape((DP * PIECE, T), BF), shape((8, T), F32)),
        [], "scale_gram", pieces.reshape(DP * PIECE, T),
    )
    mine = lax.all_to_all(low.reshape(DP, PIECE, T), "dp", 0, 0).reshape(DP * PIECE, T)
    other = lax.ppermute(mine, "core", swap)
    square_r, square_l = pltpu.VMEM((R, R), BF), pltpu.VMEM((LP, LP), BF)
    update_r, update_l = call(
        update_kernel,
        (shape((ROWS, R), F32), shape((ROWS, L), F32)),
        [pltpu.VMEM((2, DP * PIECE, T), F32)] + [square_r, square_l] * 5,
        "chain_apply", mine, other, magnitude, nest_r, nest_l,
    )
    return new_r, new_l, update_r, update_l


def solution(mesh):
    inner = Mesh(mesh.devices.reshape(DP, 4, 2), ("dp", "x", "core"))
    group = ("x", "core")
    return jax.shard_map(
        local,
        mesh=inner,
        in_specs=(P(group, "dp", None), P(group, "dp", None), P("dp", None), P("dp", None)),
        out_specs=(P("dp", None),) * 4,
        check_vma=False,
    )
```

time: 552 us -> 91.3 us (0.17)
  the two profiles are of different devices: /device:TPU:2 before, /device:TPU:1 now
where the time goes in v2:
time: 91.3 us; the launch traced here: 91 us
  blocking collectives  58.4 us (64%)
  starting transfers between devices  16.1 us (18%)
  Pallas kernels  11.2 us (12%)
  waiting for transfers between devices  2.73 us (3%)
  local copies, waits for them, and re-layouts  1.89 us (2%)
    all_to_all x1, blocking collectives, local(): pieces = lax.all_to_all(payload.reshape(DP, PIECE, T), 'dp', 0, 0)  24.6 us
    all_to_all x1, blocking collectives, local(): lax.all_to_all(low.reshape(DP, PIECE, T), 'dp', 0, 0).reshape(DP * PIECE, T)  17.9 us
    all_to_all x1, blocking collectives, local(): parts = lax.all_to_all(chip, 'x', 0, 0)  16 us
    pallas_call x4, Pallas kernels, call(): pl.pallas_call(kernel, out_shape=out_shape, in_specs=[VMEM] * len(args),...  11.2 us
    ppermute x1, starting transfers between devices, local(): latent_other = lax.ppermute(latent, 'core', swap)  8.79 us
    ppermute x1, starting transfers between devices, local(): other = lax.ppermute(mine, 'core', swap)  5.38 us
    ppermute x1, starting transfers between devices, local(): router_other = lax.ppermute(router, 'core', swap)  1.92 us
    unnamed x8, local copies, waits for them, and re-layouts  1.89 us
  transfers between devices with their start and end apart: 3, of which 2 were waited for; matrix products, arithmetic and copies ran while one was open for 0% of the time, Pallas kernels for 0%

profile of v2, /device:TPU:1, one launch (start us, length us, event | category | flops | bytes accessed | tf_op | source)
XLA Modules:
  0.0 91.0 jit_solution(15133470123883726251)
XLA Ops:
  0.6 8.8 %collective-permute-start.1 = (f32[112,576]{1,0:T(8,128)}, f32[112,576]{1,0:T(8,128)S(1)}, u32[]{:S(2)}, u32[]{:S(2)}) collective-permute-start(f32[112,576]{1,0:T(8,128)} %bitcast.9), channel_id=1, source_target_pairs={{0,1},{1,0},{2,3},{3,2},{4,5},{5,4},{6,7},{7,6},{8,9},{9,8},{10,11... | collective-permute-start | bytes 774152 | tf_op jit(solution)/shard_map/ppermute | solution.py:292
  9.4 1.9 %collective-permute-start = (f32[112,384]{1,0:T(8,128)}, f32[112,384]{1,0:T(8,128)S(1)}, u32[]{:S(2)}, u32[]{:S(2)}) collective-permute-start(f32[112,384]{1,0:T(8,128)} %bitcast.13), channel_id=1, source_target_pairs={{0,1},{1,0},{2,3},{3,2},{4,5},{5,4},{6,7},{7,6},{8,9},{9,8},{10,11... | collective-permute-start | bytes 516104 | tf_op jit(solution)/shard_map/ppermute | solution.py:291
  11.4 1.6 %collective-permute-done.router_other = f32[112,384]{1,0:T(8,128)S(1)} collective-permute-done((f32[112,384]{1,0:T(8,128)}, f32[112,384]{1,0:T(8,128)S(1)}, u32[]{:S(2)}, u32[]{:S(2)}) %collective-permute-start) | collective-permute-done | bytes 172064 | tf_op jit(solution)/shard_map/ppermute | solution.py:291
  12.9 0.0 collective-permute-done.1.latent_other
  12.9 0.0 copy-start
  12.9 1.0 %copy-done = f32[1,112,576]{2,1,0:T(8,128)S(1)} copy-done((f32[1,112,576]{2,1,0:T(8,128)S(1)}, f32[1,112,576]{2,1,0:T(8,128)}, u32[]{:S(2)}) %copy-start) | copy-done | bytes 258072
  13.9 0.0 copy-start.2
  13.9 0.9 %copy-done.2 = f32[1,112,384]{2,1,0:T(8,128)S(1)} copy-done((f32[1,112,384]{2,1,0:T(8,128)S(1)}, f32[1,112,384]{2,1,0:T(8,128)}, u32[]{:S(2)}) %copy-start.2) | copy-done | bytes 172056
  14.8 0.1 chip_sum.1
  14.9 0.0 copy-start.1
  14.9 0.0 copy-start.3
  14.9 16.0 %all_to_all.15.parts = bf16[4,112,960]{2,1,0:T(8,128)(2,1)S(1)} all-to-all(bf16[4,112,960]{2,1,0:T(8,128)(2,1)S(1)} %chip_sum.1), channel_id=1, replica_groups=mesh['dp'=64,'x'=4,'core'=2] {'x'}, dimensions={0} | all-to-all | bytes 1720320 | tf_op jit(solution)/shard_map/all_to_all | solution.py:297
  30.9 0.0 copy-done.1
  30.9 0.0 copy-done.3
  30.9 1.6 %momentum_gram.1 = (f32[112,384]{1,0:T(8,128)}, f32[112,576]{1,0:T(8,128)}, f32[112,384]{1,0:T(8,128)S(1)}, f32[112,576]{1,0:T(8,128)S(1)}, bf16[1024,128]{1,0:T(8,128)(2,1)S(1)}) custom-call(bf16[4,112,960]{2,1,0:T(8,128)(2,1)S(1)} %all_to_all.15.parts, f32[112,384]{1,0:T(8,128)S(1)} %copy-done.3, f32[112,576]{1,0:T(8,128)S(1)} %copy-done.1), custom_call_target="tpu_custom_call" | custom-call | tf_op jit(solution)/shard_map/momentum_gram/pallas_call | solution.py:276
  32.5 24.6 %all_to_all.16 = bf16[64,16,128]{2,1,0:T(8,128)(2,1)S(1)} all-to-all(bf16[64,16,128]{2,1,0:T(8,128)(2,1)S(1)} %bitcast.11), channel_id=1, replica_groups=mesh['dp'=64,'x'=4,'core'=2] {'dp'}, dimensions={0} | all-to-all | bytes 524288 | tf_op jit(solution)/shard_map/all_to_all | solution.py:308
  57.1 0.2 scale_gram.1
  57.3 17.9 %all_to_all.17 = bf16[64,16,128]{2,1,0:T(8,128)(2,1)S(1)} all-to-all(bf16[64,16,128]{2,1,0:T(8,128)(2,1)S(1)} %bitcast.12), channel_id=1, replica_groups=mesh['dp'=64,'x'=4,'core'=2] {'dp'}, dimensions={0} | all-to-all | bytes 524288 | tf_op jit(solution)/shard_map/all_to_all | solution.py:314
  75.2 5.4 %collective-permute-start.2 = (bf16[1024,128]{1,0:T(8,128)(2,1)S(1)}, bf16[1024,128]{1,0:T(8,128)(2,1)S(1)}, u32[]{:S(2)}, u32[]{:S(2)}) collective-permute-start(bf16[1024,128]{1,0:T(8,128)(2,1)S(1)} %bitcast.7), channel_id=1, source_target_pairs={{0,1},{1,0},{2,3},{3,2},{4,5},{5,4},{6,7},{7,6},{8,9},{9,8},{10,11... | collective-permute-start | bytes 786440 | tf_op jit(solution)/shard_map/ppermute | solution.py:315
  80.6 1.1 %collective-permute-done.2.other = bf16[1024,128]{1,0:T(8,128)(2,1)S(1)} collective-permute-done((bf16[1024,128]{1,0:T(8,128)(2,1)S(1)}, bf16[1024,128]{1,0:T(8,128)(2,1)S(1)}, u32[]{:S(2)}, u32[]{:S(2)}) %collective-permute-start.2) | collective-permute-done | bytes 262176 | tf_op jit(solution)/shard_map/ppermute | solution.py:315
  81.7 9.3 %chain_apply.1 = (f32[112,384]{1,0:T(8,128)}, f32[112,576]{1,0:T(8,128)}) custom-call(bf16[1024,128]{1,0:T(8,128)(2,1)S(1)} %bitcast.8, bf16[1024,128]{1,0:T(8,128)(2,1)S(1)} %collective-permute-done.2.other, f32[8,128]{1,0:T(8,128)S(1)} %get-tuple-element.17.magnitude, f32[112,384]{1,0:T(8,128)S(1)} %get-tuple-element.18.nest_r, ...), custom_call_target="tpu_custom_call" | custom-call | tf_op jit(solution)/shard_map/chain_apply/pallas_call | solution.py:276
Async XLA Ops:
  0.6 12.3 %collective-permute-start.1 = (f32[112,576]{1,0:T(8,128)}, f32[112,576]{1,0:T(8,128)S(1)}, u32[]{:S(2)}, u32[]{:S(2)}) collective-permute-start(f32[112,576]{1,0:T(8,128)} %bitcast.9), channel_id=1, source_target_pairs={{0,1},{1,0},{2,3},{3,2},{4,5},{5,4},{6,7},{7,6},{8,9},{9,8},{10,11... | collective-permute-start | bytes 774152 | tf_op jit(solution)/shard_map/ppermute | solution.py:292
  9.4 3.5 %collective-permute-start = (f32[112,384]{1,0:T(8,128)}, f32[112,384]{1,0:T(8,128)S(1)}, u32[]{:S(2)}, u32[]{:S(2)}) collective-permute-start(f32[112,384]{1,0:T(8,128)} %bitcast.13), channel_id=1, source_target_pairs={{0,1},{1,0},{2,3},{3,2},{4,5},{5,4},{6,7},{7,6},{8,9},{9,8},{10,11... | collective-permute-start | bytes 516104 | tf_op jit(solution)/shard_map/ppermute | solution.py:291
  12.9 1.0 %copy-start = (f32[1,112,576]{2,1,0:T(8,128)S(1)}, f32[1,112,576]{2,1,0:T(8,128)}, u32[]{:S(2)}) copy-start(f32[1,112,576]{2,1,0:T(8,128)} %param.5) | copy-start | bytes 774148
  13.9 0.9 %copy-start.2 = (f32[1,112,384]{2,1,0:T(8,128)S(1)}, f32[1,112,384]{2,1,0:T(8,128)}, u32[]{:S(2)}) copy-start(f32[1,112,384]{2,1,0:T(8,128)} %param.4) | copy-start | bytes 516100
  14.9 16.0 %copy-start.1 = (f32[112,576]{1,0:T(8,128)S(1)}, f32[112,576]{1,0:T(8,128)}, u32[]{:S(2)}) copy-start(f32[112,576]{1,0:T(8,128)} %moment_l.1) | copy-start | bytes 774148
  14.9 16.0 %copy-start.3 = (f32[112,384]{1,0:T(8,128)S(1)}, f32[112,384]{1,0:T(8,128)}, u32[]{:S(2)}) copy-start(f32[112,384]{1,0:T(8,128)} %moment_r.1) | copy-start | bytes 516100
  75.2 6.5 %collective-permute-start.2 = (bf16[1024,128]{1,0:T(8,128)(2,1)S(1)}, bf16[1024,128]{1,0:T(8,128)(2,1)S(1)}, u32[]{:S(2)}, u32[]{:S(2)}) collective-permute-start(bf16[1024,128]{1,0:T(8,128)(2,1)S(1)} %bitcast.7), channel_id=1, source_target_pairs={{0,1},{1,0},{2,3},{3,2},{4,5},{5,4},{6,7},{7,6},{8,9},{9,8},{10,11... | collective-permute-start | bytes 786440 | tf_op jit(solution)/shard_map/ppermute | solution.py:315

commit v3 on v2

--- a/solution.py
+++ b/solution.py
@@ -40,12 +40,10 @@
     return lax.broadcasted_iota(jnp.int32, shape, dim)
 
 
-def chip_sum_kernel(router, router_other, latent, latent_other, out):
-    a = (router[...] + router_other[...]).astype(BF)
-    b = (latent[...] + latent_other[...]).astype(BF)
+def chip_sum_kernel(mine, other, out):
+    total = (mine[...] + other[...]).astype(BF)
     for copy in range(4):
-        out[copy, :, :R] = a
-        out[copy, :, R:] = b
+        out[copy] = total
 
 
 def split3(value):
@@ -55,13 +53,13 @@
     return high, middle, rest - middle
 
 
-def gram_kernel(parts, moment_r, moment_l, new_r, new_l, nest_r, nest_l, payload, slabs, wide):
+def gram_kernel(parts, moment_r, moment_l, fresh_r, fresh_l, nest_r, nest_l, payload, slabs):
     core = lax.axis_index("core")
     squares = []
     grams = []
     for first, width, moment, new, nest in (
-        (0, R, moment_r, new_r, nest_r),
-        (R, L, moment_l, new_l, nest_l),
+        (0, R, moment_r, fresh_r, nest_r),
+        (R, L, moment_l, fresh_l, nest_l),
     ):
         part = [parts[k, :, first : first + width].astype(F32) for k in range(4)]
         summed = (part[0] + part[1]) + (part[2] + part[3])
@@ -150,9 +148,18 @@
 
 
 def update_kernel(
-    mine, other, magnitude, nest_r, nest_l, out_r, out_l,
+    mine, other, magnitude, nest_r, nest_l, fresh_r, fresh_l, new_r, new_l, out_r, out_l,
     halves, gram_r, gram_l, step_r, step_l, mix_r, mix_l, fac_r, fac_l, tmp_r, tmp_l,
+    value_r, value_l, sems,
 ):
+    copies = []
+
+    def write(source, target):
+        copies.append(pltpu.make_async_copy(source, target, sems.at[len(copies)]))
+        copies[-1].start()
+
+    write(fresh_r, new_r)
+    write(fresh_l, new_l)
     core = lax.axis_index("core")
     a, b = mine[...].astype(F32), other[...].astype(F32)
     first = core == 0
@@ -212,64 +219,85 @@
         for start in range(0, width, 256):
             stop = min(start + 256, width)
             acc = dot(left[:rows, :], right[:, start:stop])
-            epilogue(acc, start, stop)
+            for ref, value in epilogue(acc, 0, start, stop):
+                ref[:rows, start:stop] = value
+
+    def square(gram, rows, width, epilogue):
+        edge = (rows - 1) // 256 * 256
+        for start in range(0, edge, 256):
+            stop = start + 256
+            acc = dot(gram[:rows, :], gram[:, start:stop])
+            for ref, value in epilogue(acc, 0, start, stop):
+                ref[:rows, start:stop] = value
+                strip = value[edge:rows].astype(F32)
+                if rows - edge < T:
+                    strip = jnp.concatenate([strip, jnp.zeros((T + edge - rows, 256), F32)], axis=0)
+                ref[start:stop, edge:width] = strip.T.astype(BF)
+        acc = dot(gram[edge:rows, :], gram[:, edge:width])
+        for ref, value in epilogue(acc, edge, edge, width):
+            ref[edge:rows, edge:width] = value
 
     def chain(gram, step, mix, fac, tmp, rows, width):
         def store(ref):
-            def epilogue(acc, start, stop):
-                ref[:rows, start:stop] = acc.astype(BF)
-
-            return epilogue
-
-        for iteration in range(ITERS):
-            if iteration == 0:
-                now = gram
-            else:
-                now = step
-                product(fac, gram, rows, width, store(tmp))
-                yield
-                product(tmp, fac, rows, width, store(step))
-                yield
-
-            def mixing(acc, start, stop, now=now):
-                squared = acc.astype(BF).astype(F32)
-                value = COEF_B * now[:rows, start:stop].astype(F32) + COEF_C * squared
-                value = value.astype(BF)
-                mix[:rows, start:stop] = value
-                if iteration == 0:
-                    shape = (rows, stop - start)
-                    eye = (iota(shape, 0) == iota(shape, 1) + start).astype(F32)
-                    fac[:rows, start:stop] = (COEF_A * eye + value.astype(F32)).astype(BF)
-
-            product(now, now, rows, width, mixing)
+            return lambda acc, top, start, stop: [(ref, acc.astype(BF))]
+
+        def mixture(now, acc, top, start, stop):
+            squared = acc.astype(BF).astype(F32)
+            value = COEF_B * now[top : top + acc.shape[0], start:stop].astype(F32) + COEF_C * squared
+            return value.astype(BF)
+
+        def begin(acc, top, start, stop):
+            value = mixture(gram, acc, top, start, stop)
+            eye = (iota(acc.shape, 0) + top == iota(acc.shape, 1) + start).astype(F32)
+            return [(fac, (COEF_A * eye + value.astype(F32)).astype(BF))]
+
+        square(gram, rows, width, begin)
+        yield
+        for _ in range(ITERS - 1):
+
+            def mixing(acc, top, start, stop):
+                return [(mix, mixture(step, acc, top, start, stop))]
+
+            def blend(acc, top, start, stop, fac=fac, tmp=tmp):
+                value = COEF_A * fac[:rows, start:stop].astype(F32) + acc
+                return [(tmp, value.astype(BF))]
+
+            product(fac, gram, rows, width, store(tmp))
             yield
-            if iteration > 0:
-
-                def blend(acc, start, stop):
-                    value = COEF_A * fac[:rows, start:stop].astype(F32) + acc
-                    tmp[:rows, start:stop] = value.astype(BF)
-
-                product(mix, fac, rows, width, blend)
-                fac, tmp = tmp, fac
-                yield
+            product(tmp, fac, rows, width, store(step))
+            yield
+            product(step, step, rows, width, mixing)
+            yield
+            product(mix, fac, rows, width, blend)
+            fac, tmp = tmp, fac
+            yield
         yield fac
+
+    root = math.sqrt(D)
+    contract = (((1,), (1,)), ((), ()))
+
+    def apply(nest, magnitude, factor, rows, width, value, out):
+        scaled = (nest[...] / magnitude).astype(BF)
+        if width > rows:
+            scaled = jnp.concatenate([scaled, jnp.zeros((ROWS, width - rows), BF)], axis=1)
+        for start in range(0, rows, 256):
+            stop = min(start + 256, rows)
+            part = lax.dot_general(
+                scaled, factor[start:stop, :], contract, preferred_element_type=F32
+            )
+            value[:, start:stop] = part * root
+            write(value.at[:, start:stop], out.at[:, start:stop])
 
     chains = (
         chain(gram_r, step_r, mix_r, fac_r, tmp_r, R, R),
         chain(gram_l, step_l, mix_l, fac_l, tmp_l, L, LP),
     )
-    factors = [None, None]
     for _ in range(4 * ITERS - 2):
         factors = [next(c) for c in chains]
-    root = math.sqrt(D)
-    contract = (((1,), (1,)), ((), ()))
-    scaled = (nest_r[...] / magnitude[0:1, 0:1]).astype(BF)
-    out_r[...] = lax.dot_general(scaled, factors[0][...], contract, preferred_element_type=F32) * root
-    scaled = (nest_l[...] / magnitude[1:2, 0:1]).astype(BF)
-    scaled = jnp.concatenate([scaled, jnp.zeros((ROWS, LP - L), BF)], axis=1)
-    out_l[...] = (
-        lax.dot_general(scaled, factors[1][:L, :], contract, preferred_element_type=F32) * root
-    )
+    apply(nest_r, magnitude[0:1, 0:1], factors[0], R, R, value_r, out_r)
+    apply(nest_l, magnitude[1:2, 0:1], factors[1], L, LP, value_l, out_l)
+    for copy in copies:
+        copy.wait()
 
 
 def call(kernel, out_shape, scratch, name, *args):
@@ -284,26 +312,39 @@
     )(*args)
 
 
+def chain_call(mine, other, magnitude, nest_r, nest_l, fresh_r, fresh_l):
+    shape = jax.ShapeDtypeStruct
+    outs = (shape((ROWS, R), F32), shape((ROWS, L), F32)) * 2
+    square_r, square_l = pltpu.VMEM((R, R), BF), pltpu.VMEM((LP, LP), BF)
+    return pl.pallas_call(
+        update_kernel,
+        out_shape=outs,
+        in_specs=[VMEM] * 7,
+        out_specs=[pl.BlockSpec(memory_space=pl.ANY)] * 4,
+        scratch_shapes=[pltpu.VMEM((2, DP * PIECE, T), F32)]
+        + [square_r, square_l] * 5
+        + [pltpu.VMEM((ROWS, R), F32), pltpu.VMEM((ROWS, L), F32)]
+        + [pltpu.SemaphoreType.DMA((7,))],
+        compiler_params=PARAMS,
+        name="chain_apply",
+    )(mine, other, magnitude, nest_r, nest_l, fresh_r, fresh_l)
+
+
 def local(router_grads, latent_grads, router_moment, latent_moment):
     shape = jax.ShapeDtypeStruct
     swap = [(0, 1), (1, 0)]
-    router, latent = router_grads[0], latent_grads[0]
-    router_other = lax.ppermute(router, "core", swap)
-    latent_other = lax.ppermute(latent, "core", swap)
-    chip = call(
-        chip_sum_kernel, shape((4, ROWS, R + L), BF), [], "chip_sum",
-        router, router_other, latent, latent_other,
-    )
+    grads = lax.optimization_barrier(jnp.concatenate([router_grads[0], latent_grads[0]], axis=1))
+    other = lax.ppermute(grads, "core", swap)
+    chip = call(chip_sum_kernel, shape((4, ROWS, R + L), BF), [], "chip_sum", grads, other)
     parts = lax.all_to_all(chip, "x", 0, 0)
-    new_r, new_l, nest_r, nest_l, payload = call(
+    fresh_r, fresh_l, nest_r, nest_l, payload = call(
         gram_kernel,
         (
             shape((ROWS, R), F32), shape((ROWS, L), F32),
             shape((ROWS, R), F32), shape((ROWS, L), F32),
             shape((DP * PIECE, T), BF),
         ),
-        [pltpu.VMEM((DP * PIECE, T), F32), pltpu.VMEM((ROWS, LP), BF)],
-        "momentum_gram", parts, router_moment, latent_moment,
+        [pltpu.VMEM((DP * PIECE, T), F32)], "momentum_gram", parts, router_moment, latent_moment,
     )
     pieces = lax.all_to_all(payload.reshape(DP, PIECE, T), "dp", 0, 0)
     low, magnitude = call(
@@ -313,14 +354,7 @@
     )
     mine = lax.all_to_all(low.reshape(DP, PIECE, T), "dp", 0, 0).reshape(DP * PIECE, T)
     other = lax.ppermute(mine, "core", swap)
-    square_r, square_l = pltpu.VMEM((R, R), BF), pltpu.VMEM((LP, LP), BF)
-    update_r, update_l = call(
-        update_kernel,
-        (shape((ROWS, R), F32), shape((ROWS, L), F32)),
-        [pltpu.VMEM((2, DP * PIECE, T), F32)] + [square_r, square_l] * 5,
-        "chain_apply", mine, other, magnitude, nest_r, nest_l,
-    )
-    return new_r, new_l, update_r, update_l
+    return chain_call(mine, other, magnitude, nest_r, nest_l, fresh_r, fresh_l)
 
 
 def solution(mesh):

time: 91.3 us -> 86.2 us (0.944)
  local copies, waits for them, and re-layouts: 1.89 us -> 0.01 us
  blocking collectives: 58.4 us -> 56.6 us
  Pallas kernels: 11.2 us -> 10 us
  starting transfers between devices: 16.1 us -> 15 us
  other arithmetic: 0 us -> 1.04 us
    pallas_call x4 -> x3, Pallas kernels: 11.2 us -> 1.12 us  [call(): pl.pallas_call(kernel, out_shape=out_shape, in_specs=[VMEM] * len(args),...]
    pallas_call x0 -> x1, Pallas kernels: none -> 8.93 us  [chain_call(): pl.pallas_call(update_kernel, out_shape=outs, in_specs=[VMEM] * 7, out_sp...]
    ppermute x2 -> x1, starting transfers between devices: 10.7 us -> 8.79 us  [local(): other = lax.ppermute(grads, 'core', swap)]
    unnamed x8 -> x4, local copies, waits for them, and re-layouts: 1.89 us -> 0.01 us
    all_to_all x1, blocking collectives: 17.9 us -> 16.6 us  [local(): lax.all_to_all(low.reshape(DP, PIECE, T), 'dp', 0, 0).reshape(DP * PIECE, T)]
    concatenate x0 -> x1, other arithmetic: none -> 1.04 us  [local(): jnp.concatenate([router_grads[0], latent_grads[0]], axis=1)]
  transfers between devices with their start and end apart: 3 -> 2, of which waited for: 2 -> 2; matrix products, arithmetic and copies ran while one was open for 0% -> 0% of each run, Pallas kernels for 0% -> 0%
where the time goes in v3:
time: 86.2 us; the launch traced here: 85.9 us
  blocking collectives  56.6 us (66%)
  starting transfers between devices  15 us (17%)
  Pallas kernels  10 us (12%)
  waiting for transfers between devices  2.56 us (3%)
  other arithmetic  1.04 us (1%)
    all_to_all x1, blocking collectives, local(): pieces = lax.all_to_all(payload.reshape(DP, PIECE, T), 'dp', 0, 0)  24 us
    all_to_all x1, blocking collectives, local(): lax.all_to_all(low.reshape(DP, PIECE, T), 'dp', 0, 0).reshape(DP * PIECE, T)  16.6 us
    all_to_all x1, blocking collectives, local(): parts = lax.all_to_all(chip, 'x', 0, 0)  16 us
    pallas_call x1, Pallas kernels, chain_call(): pl.pallas_call(update_kernel, out_shape=outs, in_specs=[VMEM] * 7, out_sp...  8.93 us
    ppermute x1, starting transfers between devices, local(): other = lax.ppermute(grads, 'core', swap)  8.79 us
    ppermute x1, starting transfers between devices, local(): other = lax.ppermute(mine, 'core', swap)  6.17 us
  transfers between devices with their start and end apart: 2, of which 2 were waited for; matrix products, arithmetic and copies ran while one was open for 0% of the time, Pallas kernels for 0%

profile of v3, /device:TPU:1, one launch (start us, length us, event | category | flops | bytes accessed | tf_op | source)
XLA Modules:
  0.0 85.9 jit_solution(11194226079163860004)
XLA Ops:
  0.6 1.0 %pad_maximum_fusion.mine = f32[112,960]{1,0:T(8,128)S(1)} fusion(f32[112,576]{1,0:T(8,128)} %bitcast.11, f32[112,384]{1,0:T(8,128)} %bitcast.12), kind=kLoop, calls=%fused_computation | loop fusion | flops 107520 | bytes 860160 | tf_op jit(solution)/shard_map/concatenate | solution.py:336
  1.7 8.8 %collective-permute-start = (f32[112,960]{1,0:T(8,128)S(1)}, f32[112,960]{1,0:T(8,128)S(1)}, u32[]{:S(2)}, u32[]{:S(2)}) collective-permute-start(f32[112,960]{1,0:T(8,128)S(1)} %pad_maximum_fusion.mine), channel_id=1, source_target_pairs={{0,1},{1,0},{2,3},{3,2},{4,5},{5,4},{6,7},{7,6},{8,9},{9,8},{10,11... | collective-permute-start | bytes 1290248 | tf_op jit(solution)/shard_map/ppermute | solution.py:337
  10.5 1.4 %collective-permute-done.other = f32[112,960]{1,0:T(8,128)S(1)} collective-permute-done((f32[112,960]{1,0:T(8,128)S(1)}, f32[112,960]{1,0:T(8,128)S(1)}, u32[]{:S(2)}, u32[]{:S(2)}) %collective-permute-start) | collective-permute-done | bytes 430112 | tf_op jit(solution)/shard_map/ppermute | solution.py:337
  11.9 0.1 chip_sum.1
  12.0 0.0 copy-start
  12.0 0.0 copy-start.1
  12.0 16.0 %all_to_all.15.parts = bf16[4,112,960]{2,1,0:T(8,128)(2,1)S(1)} all-to-all(bf16[4,112,960]{2,1,0:T(8,128)(2,1)S(1)} %chip_sum.1), channel_id=1, replica_groups=mesh['dp'=64,'x'=4,'core'=2] {'x'}, dimensions={0} | all-to-all | bytes 1720320 | tf_op jit(solution)/shard_map/all_to_all | solution.py:339
  28.0 0.0 copy-done
  28.0 0.0 copy-done.1
  28.0 0.9 %momentum_gram.1 = (f32[112,384]{1,0:T(8,128)S(1)}, f32[112,576]{1,0:T(8,128)S(1)}, f32[112,384]{1,0:T(8,128)S(1)}, f32[112,576]{1,0:T(8,128)S(1)}, bf16[1024,128]{1,0:T(8,128)(2,1)S(1)}) custom-call(bf16[4,112,960]{2,1,0:T(8,128)(2,1)S(1)} %all_to_all.15.parts, f32[112,384]{1,0:T(8,128)S(1)} %copy-done.1, f32[112,576]{1,0:T(8,128)S(1)} %copy-done), custom_call_target="tpu_custom_call" | custom-call | tf_op jit(solution)/shard_map/momentum_gram/pallas_call | solution.py:304
  28.9 24.0 %all_to_all.16 = bf16[64,16,128]{2,1,0:T(8,128)(2,1)S(1)} all-to-all(bf16[64,16,128]{2,1,0:T(8,128)(2,1)S(1)} %bitcast.9), channel_id=1, replica_groups=mesh['dp'=64,'x'=4,'core'=2] {'dp'}, dimensions={0} | all-to-all | bytes 524288 | tf_op jit(solution)/shard_map/all_to_all | solution.py:349
  52.9 0.2 scale_gram.1
  53.1 16.6 %all_to_all.17 = bf16[64,16,128]{2,1,0:T(8,128)(2,1)S(1)} all-to-all(bf16[64,16,128]{2,1,0:T(8,128)(2,1)S(1)} %bitcast.10), channel_id=1, replica_groups=mesh['dp'=64,'x'=4,'core'=2] {'dp'}, dimensions={0} | all-to-all | bytes 524288 | tf_op jit(solution)/shard_map/all_to_all | solution.py:355
  69.7 6.2 %collective-permute-start.1 = (bf16[1024,128]{1,0:T(8,128)(2,1)S(1)}, bf16[1024,128]{1,0:T(8,128)(2,1)S(1)}, u32[]{:S(2)}, u32[]{:S(2)}) collective-permute-start(bf16[1024,128]{1,0:T(8,128)(2,1)S(1)} %bitcast.7), channel_id=1, source_target_pairs={{0,1},{1,0},{2,3},{3,2},{4,5},{5,4},{6,7},{7,6},{8,9},{9,8},{10,11... | collective-permute-start | bytes 786440 | tf_op jit(solution)/shard_map/ppermute | solution.py:356
  75.9 1.1 %collective-permute-done.1.other = bf16[1024,128]{1,0:T(8,128)(2,1)S(1)} collective-permute-done((bf16[1024,128]{1,0:T(8,128)(2,1)S(1)}, bf16[1024,128]{1,0:T(8,128)(2,1)S(1)}, u32[]{:S(2)}, u32[]{:S(2)}) %collective-permute-start.1) | collective-permute-done | bytes 262176 | tf_op jit(solution)/shard_map/ppermute | solution.py:356
  77.0 8.9 %chain_apply.1 = (f32[112,384]{1,0:T(8,128)}, f32[112,576]{1,0:T(8,128)}, f32[112,384]{1,0:T(8,128)}, f32[112,576]{1,0:T(8,128)}) custom-call(bf16[1024,128]{1,0:T(8,128)(2,1)S(1)} %bitcast.8, bf16[1024,128]{1,0:T(8,128)(2,1)S(1)} %collective-permute-done.1.other, f32[8,128]{1,0:T(8,128)S(1)} %get-tuple-element.13.magnitude, ...), custom_call_target="tpu_custom_call" | custom-call | tf_op jit(solution)/shard_map/chain_apply/pallas_call | solution.py:319
Async XLA Ops:
  1.7 10.2 %collective-permute-start = (f32[112,960]{1,0:T(8,128)S(1)}, f32[112,960]{1,0:T(8,128)S(1)}, u32[]{:S(2)}, u32[]{:S(2)}) collective-permute-start(f32[112,960]{1,0:T(8,128)S(1)} %pad_maximum_fusion.mine), channel_id=1, source_target_pairs={{0,1},{1,0},{2,3},{3,2},{4,5},{5,4},{6,7},{7,6},{8,9},{9,8},{10,11... | collective-permute-start | bytes 1290248 | tf_op jit(solution)/shard_map/ppermute | solution.py:337
  12.0 16.0 %copy-start = (f32[112,576]{1,0:T(8,128)S(1)}, f32[112,576]{1,0:T(8,128)}, u32[]{:S(2)}) copy-start(f32[112,576]{1,0:T(8,128)} %moment_l.1) | copy-start | bytes 774148
  12.0 16.0 %copy-start.1 = (f32[112,384]{1,0:T(8,128)S(1)}, f32[112,384]{1,0:T(8,128)}, u32[]{:S(2)}) copy-start(f32[112,384]{1,0:T(8,128)} %moment_r.1) | copy-start | bytes 516100
  69.7 7.3 %collective-permute-start.1 = (bf16[1024,128]{1,0:T(8,128)(2,1)S(1)}, bf16[1024,128]{1,0:T(8,128)(2,1)S(1)}, u32[]{:S(2)}, u32[]{:S(2)}) collective-permute-start(bf16[1024,128]{1,0:T(8,128)(2,1)S(1)} %bitcast.7), channel_id=1, source_target_pairs={{0,1},{1,0},{2,3},{3,2},{4,5},{5,4},{6,7},{7,6},{8,9},{9,8},{10,11... | collective-permute-start | bytes 786440 | tf_op jit(solution)/shard_map/ppermute | solution.py:356

commit v4 on v3

--- a/solution.py
+++ b/solution.py
@@ -215,29 +215,31 @@
     for ref in (step_l, mix_l, fac_l, tmp_l):
         ref[L:, :] = jnp.zeros((LP - L, LP), BF)
 
-    def product(left, right, rows, width, epilogue):
+    def product(left, right, rows, width, epilogue, symmetric=False):
+        if symmetric:
+            return mirrored(left, right, rows, width, epilogue)
         for start in range(0, width, 256):
             stop = min(start + 256, width)
             acc = dot(left[:rows, :], right[:, start:stop])
             for ref, value in epilogue(acc, 0, start, stop):
                 ref[:rows, start:stop] = value
 
-    def square(gram, rows, width, epilogue):
+    def mirrored(left, right, rows, width, epilogue):
         edge = (rows - 1) // 256 * 256
         for start in range(0, edge, 256):
             stop = start + 256
-            acc = dot(gram[:rows, :], gram[:, start:stop])
+            acc = dot(left[:rows, :], right[:, start:stop])
             for ref, value in epilogue(acc, 0, start, stop):
                 ref[:rows, start:stop] = value
                 strip = value[edge:rows].astype(F32)
                 if rows - edge < T:
                     strip = jnp.concatenate([strip, jnp.zeros((T + edge - rows, 256), F32)], axis=0)
                 ref[start:stop, edge:width] = strip.T.astype(BF)
-        acc = dot(gram[edge:rows, :], gram[:, edge:width])
+        acc = dot(left[edge:rows, :], right[:, edge:width])
         for ref, value in epilogue(acc, edge, edge, width):
             ref[edge:rows, edge:width] = value
 
-    def chain(gram, step, mix, fac, tmp, rows, width):
+    def chain(gram, step, mix, fac, tmp, rows, width, mirror):
         def store(ref):
             return lambda acc, top, start, stop: [(ref, acc.astype(BF))]
 
@@ -251,24 +253,24 @@
             eye = (iota(acc.shape, 0) + top == iota(acc.shape, 1) + start).astype(F32)
             return [(fac, (COEF_A * eye + value.astype(F32)).astype(BF))]
 
-        square(gram, rows, width, begin)
+        mirrored(gram, gram, rows, width, begin)
         yield
-        for _ in range(ITERS - 1):
+        for it in range(ITERS - 1):
 
             def mixing(acc, top, start, stop):
                 return [(mix, mixture(step, acc, top, start, stop))]
 
             def blend(acc, top, start, stop, fac=fac, tmp=tmp):
-                value = COEF_A * fac[:rows, start:stop].astype(F32) + acc
+                value = COEF_A * fac[top : top + acc.shape[0], start:stop].astype(F32) + acc
                 return [(tmp, value.astype(BF))]
 
-            product(fac, gram, rows, width, store(tmp))
+            product(fac, gram, rows, width, store(tmp), mirror and it == 0)
             yield
-            product(tmp, fac, rows, width, store(step))
+            product(tmp, fac, rows, width, store(step), mirror)
             yield
-            product(step, step, rows, width, mixing)
+            product(step, step, rows, width, mixing, mirror)
             yield
-            product(mix, fac, rows, width, blend)
+            product(mix, fac, rows, width, blend, mirror)
             fac, tmp = tmp, fac
             yield
         yield fac
@@ -289,8 +291,8 @@
             write(value.at[:, start:stop], out.at[:, start:stop])
 
     chains = (
-        chain(gram_r, step_r, mix_r, fac_r, tmp_r, R, R),
-        chain(gram_l, step_l, mix_l, fac_l, tmp_l, L, LP),
+        chain(gram_r, step_r, mix_r, fac_r, tmp_r, R, R, False),
+        chain(gram_l, step_l, mix_l, fac_l, tmp_l, L, LP, True),
     )
     for _ in range(4 * ITERS - 2):
         factors = [next(c) for c in chains]

time: 86.2 us -> 85.3 us (0.990)
  Pallas kernels: 10 us -> 9.08 us
    pallas_call x1, Pallas kernels: 8.93 us -> 7.96 us  [chain_call(): pl.pallas_call(update_kernel, out_shape=outs, in_specs=[VMEM] * 7, out_sp...]
where the time goes in v4:
time: 85.3 us; the launch traced here: 85 us
  blocking collectives  56.6 us (66%)
  starting transfers between devices  15 us (18%)
  Pallas kernels  9.08 us (11%)
  waiting for transfers between devices  2.56 us (3%)
  other arithmetic  1.04 us (1%)
    all_to_all x1, blocking collectives, local(): pieces = lax.all_to_all(payload.reshape(DP, PIECE, T), 'dp', 0, 0)  24 us
    all_to_all x1, blocking collectives, local(): lax.all_to_all(low.reshape(DP, PIECE, T), 'dp', 0, 0).reshape(DP * PIECE, T)  16.6 us
    all_to_all x1, blocking collectives, local(): parts = lax.all_to_all(chip, 'x', 0, 0)  16 us
    ppermute x1, starting transfers between devices, local(): other = lax.ppermute(grads, 'core', swap)  8.79 us
    pallas_call x1, Pallas kernels, chain_call(): pl.pallas_call(update_kernel, out_shape=outs, in_specs=[VMEM] * 7, out_sp...  7.96 us
    ppermute x1, starting transfers between devices, local(): other = lax.ppermute(mine, 'core', swap)  6.17 us
  transfers between devices with their start and end apart: 2, of which 2 were waited for; matrix products, arithmetic and copies ran while one was open for 0% of the time, Pallas kernels for 0%

profile of v4, /device:TPU:1, one launch (start us, length us, event | category | flops | bytes accessed | tf_op | source)
XLA Modules:
  0.0 85.0 jit_solution(5333975974557052381)
XLA Ops:
  0.6 1.0 %pad_maximum_fusion.mine = f32[112,960]{1,0:T(8,128)S(1)} fusion(f32[112,576]{1,0:T(8,128)} %bitcast.11, f32[112,384]{1,0:T(8,128)} %bitcast.12), kind=kLoop, calls=%fused_computation | loop fusion | flops 107520 | bytes 860160 | tf_op jit(solution)/shard_map/concatenate | solution.py:338
  1.7 8.8 %collective-permute-start = (f32[112,960]{1,0:T(8,128)S(1)}, f32[112,960]{1,0:T(8,128)S(1)}, u32[]{:S(2)}, u32[]{:S(2)}) collective-permute-start(f32[112,960]{1,0:T(8,128)S(1)} %pad_maximum_fusion.mine), channel_id=1, source_target_pairs={{0,1},{1,0},{2,3},{3,2},{4,5},{5,4},{6,7},{7,6},{8,9},{9,8},{10,11... | collective-permute-start | bytes 1290248 | tf_op jit(solution)/shard_map/ppermute | solution.py:339
  10.5 1.4 %collective-permute-done.other = f32[112,960]{1,0:T(8,128)S(1)} collective-permute-done((f32[112,960]{1,0:T(8,128)S(1)}, f32[112,960]{1,0:T(8,128)S(1)}, u32[]{:S(2)}, u32[]{:S(2)}) %collective-permute-start) | collective-permute-done | bytes 430112 | tf_op jit(solution)/shard_map/ppermute | solution.py:339
  11.9 0.1 chip_sum.1
  12.0 0.0 copy-start
  12.0 0.0 copy-start.1
  12.0 16.0 %all_to_all.15.parts = bf16[4,112,960]{2,1,0:T(8,128)(2,1)S(1)} all-to-all(bf16[4,112,960]{2,1,0:T(8,128)(2,1)S(1)} %chip_sum.1), channel_id=1, replica_groups=mesh['dp'=64,'x'=4,'core'=2] {'x'}, dimensions={0} | all-to-all | bytes 1720320 | tf_op jit(solution)/shard_map/all_to_all | solution.py:341
  28.0 0.0 copy-done
  28.0 0.0 copy-done.1
  28.0 0.9 %momentum_gram.1 = (f32[112,384]{1,0:T(8,128)S(1)}, f32[112,576]{1,0:T(8,128)S(1)}, f32[112,384]{1,0:T(8,128)S(1)}, f32[112,576]{1,0:T(8,128)S(1)}, bf16[1024,128]{1,0:T(8,128)(2,1)S(1)}) custom-call(bf16[4,112,960]{2,1,0:T(8,128)(2,1)S(1)} %all_to_all.15.parts, f32[112,384]{1,0:T(8,128)S(1)} %copy-done.1, f32[112,576]{1,0:T(8,128)S(1)} %copy-done), custom_call_target="tpu_custom_call" | custom-call | tf_op jit(solution)/shard_map/momentum_gram/pallas_call | solution.py:306
  28.9 24.0 %all_to_all.16 = bf16[64,16,128]{2,1,0:T(8,128)(2,1)S(1)} all-to-all(bf16[64,16,128]{2,1,0:T(8,128)(2,1)S(1)} %bitcast.9), channel_id=1, replica_groups=mesh['dp'=64,'x'=4,'core'=2] {'dp'}, dimensions={0} | all-to-all | bytes 524288 | tf_op jit(solution)/shard_map/all_to_all | solution.py:351
  52.9 0.2 scale_gram.1
  53.1 16.6 %all_to_all.17 = bf16[64,16,128]{2,1,0:T(8,128)(2,1)S(1)} all-to-all(bf16[64,16,128]{2,1,0:T(8,128)(2,1)S(1)} %bitcast.10), channel_id=1, replica_groups=mesh['dp'=64,'x'=4,'core'=2] {'dp'}, dimensions={0} | all-to-all | bytes 524288 | tf_op jit(solution)/shard_map/all_to_all | solution.py:357
  69.7 6.2 %collective-permute-start.1 = (bf16[1024,128]{1,0:T(8,128)(2,1)S(1)}, bf16[1024,128]{1,0:T(8,128)(2,1)S(1)}, u32[]{:S(2)}, u32[]{:S(2)}) collective-permute-start(bf16[1024,128]{1,0:T(8,128)(2,1)S(1)} %bitcast.7), channel_id=1, source_target_pairs={{0,1},{1,0},{2,3},{3,2},{4,5},{5,4},{6,7},{7,6},{8,9},{9,8},{10,11... | collective-permute-start | bytes 786440 | tf_op jit(solution)/shard_map/ppermute | solution.py:358
  75.9 1.1 %collective-permute-done.1.other = bf16[1024,128]{1,0:T(8,128)(2,1)S(1)} collective-permute-done((bf16[1024,128]{1,0:T(8,128)(2,1)S(1)}, bf16[1024,128]{1,0:T(8,128)(2,1)S(1)}, u32[]{:S(2)}, u32[]{:S(2)}) %collective-permute-start.1) | collective-permute-done | bytes 262176 | tf_op jit(solution)/shard_map/ppermute | solution.py:358
  77.0 8.0 %chain_apply.1 = (f32[112,384]{1,0:T(8,128)}, f32[112,576]{1,0:T(8,128)}, f32[112,384]{1,0:T(8,128)}, f32[112,576]{1,0:T(8,128)}) custom-call(bf16[1024,128]{1,0:T(8,128)(2,1)S(1)} %bitcast.8, bf16[1024,128]{1,0:T(8,128)(2,1)S(1)} %collective-permute-done.1.other, f32[8,128]{1,0:T(8,128)S(1)} %get-tuple-element.13.magnitude, ...), custom_call_target="tpu_custom_call" | custom-call | tf_op jit(solution)/shard_map/chain_apply/pallas_call | solution.py:321
Async XLA Ops:
  1.7 10.2 %collective-permute-start = (f32[112,960]{1,0:T(8,128)S(1)}, f32[112,960]{1,0:T(8,128)S(1)}, u32[]{:S(2)}, u32[]{:S(2)}) collective-permute-start(f32[112,960]{1,0:T(8,128)S(1)} %pad_maximum_fusion.mine), channel_id=1, source_target_pairs={{0,1},{1,0},{2,3},{3,2},{4,5},{5,4},{6,7},{7,6},{8,9},{9,8},{10,11... | collective-permute-start | bytes 1290248 | tf_op jit(solution)/shard_map/ppermute | solution.py:339
  12.0 16.0 %copy-start = (f32[112,576]{1,0:T(8,128)S(1)}, f32[112,576]{1,0:T(8,128)}, u32[]{:S(2)}) copy-start(f32[112,576]{1,0:T(8,128)} %moment_l.1) | copy-start | bytes 774148
  12.0 16.0 %copy-start.1 = (f32[112,384]{1,0:T(8,128)S(1)}, f32[112,384]{1,0:T(8,128)}, u32[]{:S(2)}) copy-start(f32[112,384]{1,0:T(8,128)} %moment_r.1) | copy-start | bytes 516100
  69.7 7.3 %collective-permute-start.1 = (bf16[1024,128]{1,0:T(8,128)(2,1)S(1)}, bf16[1024,128]{1,0:T(8,128)(2,1)S(1)}, u32[]{:S(2)}, u32[]{:S(2)}) collective-permute-start(bf16[1024,128]{1,0:T(8,128)(2,1)S(1)} %bitcast.7), channel_id=1, source_target_pairs={{0,1},{1,0},{2,3},{3,2},{4,5},{5,4},{6,7},{7,6},{8,9},{9,8},{10,11... | collective-permute-start | bytes 786440 | tf_op jit(solution)/shard_map/ppermute | solution.py:358

commit v5 on v4

--- a/solution.py
+++ b/solution.py
@@ -120,7 +120,7 @@
         @pl.when(core == c)
         def _():
             for s in range(SLABS):
-                slabs[pl.ds(s, DP, stride=PIECE), :] = pieces[SLABS * c + s]
+                slabs[pl.ds(s, DP, stride=PIECE), :] = pieces[SLABS * (1 - c) + s]
 
     slabs[pl.ds(SLABS, DP, stride=PIECE), :] = extra
     payload[...] = slabs[...].astype(BF)
@@ -138,7 +138,7 @@
     inverse_r = 1.0 / (router * router)
     inverse_l = 1.0 / (latent * latent)
     row, lane = iota((PIECE, T), 0), iota((PIECE, T), 1)
-    slab = SLABS * core + row
+    slab = SLABS * (1 - core) + row
     of_router = (slab < 9) | ((slab == 9) & (lane >= 64))
     of_router = jnp.where(row == SLABS, jnp.where(here < 2, 1, 0), jnp.where(of_router, 1, 0))
     scaled = (total * jnp.where(of_router == 1, inverse_r, inverse_l)).astype(BF)
@@ -147,24 +147,10 @@
     magnitude[...] = jnp.where(iota((8, T), 0) == 0, router, latent)
 
 
-def update_kernel(
-    mine, other, magnitude, nest_r, nest_l, fresh_r, fresh_l, new_r, new_l, out_r, out_l,
-    halves, gram_r, gram_l, step_r, step_l, mix_r, mix_l, fac_r, fac_l, tmp_r, tmp_l,
-    value_r, value_l, sems,
-):
-    copies = []
-
-    def write(source, target):
-        copies.append(pltpu.make_async_copy(source, target, sems.at[len(copies)]))
-        copies[-1].start()
-
-    write(fresh_r, new_r)
-    write(fresh_l, new_l)
-    core = lax.axis_index("core")
-    a, b = mine[...].astype(F32), other[...].astype(F32)
-    first = core == 0
-    halves[0] = jnp.where(first, a, b)
-    halves[1] = jnp.where(first, b, a)
+def unpacker(halves):
+    row, lane = iota((T, T), 0), iota((T, T), 1)
+    lane1 = iota((1, T), 1)
+    extra = halves[0, pl.ds(SLABS, 8, stride=PIECE), :]
 
     def slab(g):
         return halves[g // SLABS, pl.ds(g % SLABS, DP, stride=PIECE), :]
@@ -175,15 +161,13 @@
     def put(ref, i, j, value):
         ref[T * i : T * (i + 1), T * j : T * (j + 1)] = value.astype(BF)
 
-    extra = halves[0, pl.ds(SLABS, 8, stride=PIECE), :]
-    row, lane = iota((T, T), 0), iota((T, T), 1)
-    lane1 = iota((1, T), 1)
-
-    def both(ref, i, j, value):
+    def both(ref, i, j, t):
+        value = tile(t)
         put(ref, i, j, value)
         put(ref, j, i, value.T)
 
-    def unfold(ref, i, j, value, k):
+    def unfold(ref, i, j, t, k):
+        value = tile(t)
         flipped = value.T
         put(ref, i, i, jnp.where(row <= lane, value, flipped))
         low_half = pltpu.roll(extra[2 * k : 2 * k + 1], 64, 1)
@@ -191,89 +175,113 @@
         inner = jnp.where(row > lane, value, flipped)
         put(ref, j, j, jnp.where(row == lane, diagonal, inner))
 
-    both(gram_r, 0, 1, tile(0))
-    both(gram_r, 0, 2, tile(1))
-    both(gram_r, 1, 2, tile(2))
-    unfold(gram_r, 0, 1, tile(3), 0)
-    last = tile(4)
-    put(gram_r, 2, 2, jnp.where(row <= lane, last, last.T))
-    gram_l[L:, :] = jnp.zeros((LP - L, LP), BF)
-    gram_l[512:L, 512:] = jnp.where(iota((64, T), 1) < 64, last[64:], 0.0).astype(BF)
-    both(gram_l, 0, 1, tile(5))
-    both(gram_l, 0, 2, tile(6))
-    both(gram_l, 0, 3, tile(7))
-    both(gram_l, 1, 2, tile(8))
-    both(gram_l, 1, 3, tile(9))
-    both(gram_l, 2, 3, tile(10))
-    unfold(gram_l, 0, 1, tile(11), 1)
-    unfold(gram_l, 2, 3, tile(12), 2)
-    for j in range(4):
-        strip = jnp.concatenate([slab(26 + j), jnp.zeros((64, T), F32)], axis=0)
-        gram_l[512:L, T * j : T * (j + 1)] = strip[:64].astype(BF)
-        put(gram_l, j, 4, strip.T)
-
-    for ref in (step_l, mix_l, fac_l, tmp_l):
-        ref[L:, :] = jnp.zeros((LP - L, LP), BF)
-
-    def product(left, right, rows, width, epilogue, symmetric=False):
-        if symmetric:
-            return mirrored(left, right, rows, width, epilogue)
-        for start in range(0, width, 256):
-            stop = min(start + 256, width)
-            acc = dot(left[:rows, :], right[:, start:stop])
-            for ref, value in epilogue(acc, 0, start, stop):
-                ref[:rows, start:stop] = value
-
-    def mirrored(left, right, rows, width, epilogue):
-        edge = (rows - 1) // 256 * 256
-        for start in range(0, edge, 256):
-            stop = start + 256
-            acc = dot(left[:rows, :], right[:, start:stop])
-            for ref, value in epilogue(acc, 0, start, stop):
-                ref[:rows, start:stop] = value
+    return slab, tile, put, both, unfold
+
+
+def product(left, right, rows, width, epilogue, symmetric=False):
+    edge = (rows - 1) // 256 * 256 if symmetric else width
+    for start in range(0, edge, 256):
+        stop = min(start + 256, edge)
+        acc = dot(left[:rows, :], right[:, start:stop])
+        for ref, value in epilogue(acc, 0, start, stop):
+            ref[:rows, start:stop] = value
+            if symmetric:
                 strip = value[edge:rows].astype(F32)
                 if rows - edge < T:
                     strip = jnp.concatenate([strip, jnp.zeros((T + edge - rows, 256), F32)], axis=0)
                 ref[start:stop, edge:width] = strip.T.astype(BF)
+    if symmetric:
         acc = dot(left[edge:rows, :], right[:, edge:width])
         for ref, value in epilogue(acc, edge, edge, width):
             ref[edge:rows, edge:width] = value
 
-    def chain(gram, step, mix, fac, tmp, rows, width, mirror):
-        def store(ref):
-            return lambda acc, top, start, stop: [(ref, acc.astype(BF))]
-
-        def mixture(now, acc, top, start, stop):
-            squared = acc.astype(BF).astype(F32)
-            value = COEF_B * now[top : top + acc.shape[0], start:stop].astype(F32) + COEF_C * squared
-            return value.astype(BF)
-
-        def begin(acc, top, start, stop):
-            value = mixture(gram, acc, top, start, stop)
-            eye = (iota(acc.shape, 0) + top == iota(acc.shape, 1) + start).astype(F32)
-            return [(fac, (COEF_A * eye + value.astype(F32)).astype(BF))]
-
-        mirrored(gram, gram, rows, width, begin)
-        yield
-        for it in range(ITERS - 1):
-
-            def mixing(acc, top, start, stop):
-                return [(mix, mixture(step, acc, top, start, stop))]
-
-            def blend(acc, top, start, stop, fac=fac, tmp=tmp):
-                value = COEF_A * fac[top : top + acc.shape[0], start:stop].astype(F32) + acc
-                return [(tmp, value.astype(BF))]
-
-            product(fac, gram, rows, width, store(tmp), mirror and it == 0)
-            yield
-            product(tmp, fac, rows, width, store(step), mirror)
-            yield
-            product(step, step, rows, width, mixing, mirror)
-            yield
-            product(mix, fac, rows, width, blend, mirror)
-            fac, tmp = tmp, fac
-            yield
-        yield fac
+
+def chain(gram, step, mix, fac, tmp, rows, width, symmetric):
+    def store(ref):
+        return lambda acc, top, start, stop: [(ref, acc.astype(BF))]
+
+    def mixture(now, acc, top, start, stop):
+        squared = acc.astype(BF).astype(F32)
+        value = COEF_B * now[top : top + acc.shape[0], start:stop].astype(F32) + COEF_C * squared
+        return value.astype(BF)
+
+    def begin(acc, top, start, stop):
+        value = mixture(gram, acc, top, start, stop)
+        eye = (iota(acc.shape, 0) + top == iota(acc.shape, 1) + start).astype(F32)
+        return [(fac, (COEF_A * eye + value.astype(F32)).astype(BF))]
+
+    product(gram, gram, rows, width, begin, True)
+    for iteration in range(1, ITERS):
+
+        def mixing(acc, top, start, stop):
+            return [(mix, mixture(step, acc, top, start, stop))]
+
+        def blend(acc, top, start, stop, fac=fac, tmp=tmp):
+            value = COEF_A * fac[top : top + acc.shape[0], start:stop].astype(F32) + acc
+            return [(tmp, value.astype(BF))]
+
+        product(fac, gram, rows, width, store(tmp), symmetric and iteration == 1)
+        product(tmp, fac, rows, width, store(step), symmetric)
+        product(step, step, rows, width, mixing, symmetric)
+        product(mix, fac, rows, width, blend, symmetric)
+        fac, tmp = tmp, fac
+    return fac
+
+
+def router_kernel(mine, out, half, gram, step, mix, fac, tmp):
+    out[: DP * PIECE, :] = mine[...]
+
+    @pl.when(lax.axis_index("core") == 1)
+    def _():
+        half[0] = mine[...].astype(F32)
+        slab, tile, put, both, unfold = unpacker(half)
+        both(gram, 0, 1, 0)
+        both(gram, 0, 2, 1)
+        both(gram, 1, 2, 2)
+        unfold(gram, 0, 1, 3, 0)
+        last = tile(4)
+        upper = iota((T, T), 0) <= iota((T, T), 1)
+        put(gram, 2, 2, jnp.where(upper, last, last.T))
+        factor = chain(gram, step, mix, fac, tmp, R, R, False)
+        for j in range(R // T):
+            first = DP * PIECE + R * j
+            out[first : first + R, :] = factor[:, T * j : T * (j + 1)]
+
+
+def update_kernel(
+    mine, other, magnitude, nest_r, nest_l, fresh_r, fresh_l, new_r, new_l, out_r, out_l,
+    halves, gram, step, mix, fac, tmp, fac_r, value_r, value_l, sems,
+):
+    copies = []
+
+    def write(source, target):
+        copies.append(pltpu.make_async_copy(source, target, sems.at[len(copies)]))
+        copies[-1].start()
+
+    write(fresh_r, new_r)
+    write(fresh_l, new_l)
+
+    first = lax.axis_index("core") == 1
+    a, b = mine[: DP * PIECE, :].astype(F32), other[: DP * PIECE, :].astype(F32)
+    halves[0] = jnp.where(first, a, b)
+    halves[1] = jnp.where(first, b, a)
+    slab, tile, put, both, unfold = unpacker(halves)
+    gram[L:, :] = jnp.zeros((LP - L, LP), BF)
+    gram[512:L, 512:] = jnp.where(iota((64, T), 1) < 64, slab(9), 0.0).astype(BF)
+    both(gram, 0, 1, 5)
+    both(gram, 0, 2, 6)
+    both(gram, 0, 3, 7)
+    both(gram, 1, 2, 8)
+    both(gram, 1, 3, 9)
+    both(gram, 2, 3, 10)
+    unfold(gram, 0, 1, 11, 1)
+    unfold(gram, 2, 3, 12, 2)
+    for j in range(4):
+        strip = jnp.concatenate([slab(26 + j), jnp.zeros((64, T), F32)], axis=0)
+        gram[512:L, T * j : T * (j + 1)] = strip[:64].astype(BF)
+        put(gram, j, 4, strip.T)
+    for ref in (step, mix, fac, tmp):
+        ref[L:, :] = jnp.zeros((LP - L, LP), BF)
 
     root = math.sqrt(D)
     contract = (((1,), (1,)), ((), ()))
@@ -290,14 +298,12 @@
             value[:, start:stop] = part * root
             write(value.at[:, start:stop], out.at[:, start:stop])
 
-    chains = (
-        chain(gram_r, step_r, mix_r, fac_r, tmp_r, R, R, False),
-        chain(gram_l, step_l, mix_l, fac_l, tmp_l, L, LP, True),
-    )
-    for _ in range(4 * ITERS - 2):
-        factors = [next(c) for c in chains]
-    apply(nest_r, magnitude[0:1, 0:1], factors[0], R, R, value_r, out_r)
-    apply(nest_l, magnitude[1:2, 0:1], factors[1], L, LP, value_l, out_l)
+    for j in range(R // T):
+        rows = slice(DP * PIECE + R * j, DP * PIECE + R * (j + 1))
+        fac_r[:, T * j : T * (j + 1)] = jnp.where(first, mine[rows, :], other[rows, :])
+    apply(nest_r, magnitude[0:1, 0:1], fac_r, R, R, value_r, out_r)
+    factor = chain(gram, step, mix, fac, tmp, L, LP, True)
+    apply(nest_l, magnitude[1:2, 0:1], factor, L, LP, value_l, out_l)
     for copy in copies:
         copy.wait()
 
@@ -314,18 +320,25 @@
     )(*args)
 
 
+def router_call(mine):
+    return call(
+        router_kernel,
+        jax.ShapeDtypeStruct((DP * PIECE + R * R // T, T), BF),
+        [pltpu.VMEM((1, DP * PIECE, T), F32)] + [pltpu.VMEM((R, R), BF)] * 5,
+        "router_chain", mine,
+    )
+
+
 def chain_call(mine, other, magnitude, nest_r, nest_l, fresh_r, fresh_l):
     shape = jax.ShapeDtypeStruct
-    outs = (shape((ROWS, R), F32), shape((ROWS, L), F32)) * 2
-    square_r, square_l = pltpu.VMEM((R, R), BF), pltpu.VMEM((LP, LP), BF)
     return pl.pallas_call(
         update_kernel,
-        out_shape=outs,
+        out_shape=(shape((ROWS, R), F32), shape((ROWS, L), F32)) * 2,
         in_specs=[VMEM] * 7,
         out_specs=[pl.BlockSpec(memory_space=pl.ANY)] * 4,
         scratch_shapes=[pltpu.VMEM((2, DP * PIECE, T), F32)]
-        + [square_r, square_l] * 5
-        + [pltpu.VMEM((ROWS, R), F32), pltpu.VMEM((ROWS, L), F32)]
+        + [pltpu.VMEM((LP, LP), BF)] * 5
+        + [pltpu.VMEM((R, R), BF), pltpu.VMEM((ROWS, R), F32), pltpu.VMEM((ROWS, L), F32)]
         + [pltpu.SemaphoreType.DMA((7,))],
         compiler_params=PARAMS,
         name="chain_apply",
@@ -355,6 +368,7 @@
         [], "scale_gram", pieces.reshape(DP * PIECE, T),
     )
     mine = lax.all_to_all(low.reshape(DP, PIECE, T), "dp", 0, 0).reshape(DP * PIECE, T)
+    mine = router_call(mine)
     other = lax.ppermute(mine, "core", swap)
     return chain_call(mine, other, magnitude, nest_r, nest_l, fresh_r, fresh_l)
 

time: 85.3 us -> 84.6 us (level)
  starting transfers between devices: 15 us -> 11.4 us
  Pallas kernels: 9.08 us -> 10.6 us
  blocking collectives: 56.6 us -> 57.5 us
    ppermute x1, starting transfers between devices: 6.17 us -> 2.65 us  [local(): other = lax.ppermute(mine, 'core', swap)]
    pallas_call x3 -> x4, Pallas kernels: 1.12 us -> 3.95 us  [call(): pl.pallas_call(kernel, out_shape=out_shape, in_specs=[VMEM] * len(args),...]
    pallas_call x1, Pallas kernels: 7.96 us -> 6.64 us  [chain_call(): pl.pallas_call(update_kernel, out_shape=(shape((ROWS, R), F32), shape((RO...]
where the time goes in v5:
time: 84.6 us; the launch traced here: 84.3 us
  blocking collectives  57.5 us (68%)
  starting transfers between devices  11.4 us (13%)
  Pallas kernels  10.6 us (13%)
  waiting for transfers between devices  2.98 us (4%)
  other arithmetic  1.04 us (1%)
    all_to_all x1, blocking collectives, local(): pieces = lax.all_to_all(payload.reshape(DP, PIECE, T), 'dp', 0, 0)  24.2 us
    all_to_all x1, blocking collectives, local(): lax.all_to_all(low.reshape(DP, PIECE, T), 'dp', 0, 0).reshape(DP * PIECE, T)  17.3 us
    all_to_all x1, blocking collectives, local(): parts = lax.all_to_all(chip, 'x', 0, 0)  16 us
    ppermute x1, starting transfers between devices, local(): other = lax.ppermute(grads, 'core', swap)  8.79 us
    pallas_call x1, Pallas kernels, chain_call(): pl.pallas_call(update_kernel, out_shape=(shape((ROWS, R), F32), shape((RO...  6.64 us
    pallas_call x4, Pallas kernels, call(): pl.pallas_call(kernel, out_shape=out_shape, in_specs=[VMEM] * len(args),...  3.95 us
    ppermute x1, starting transfers between devices, local(): other = lax.ppermute(mine, 'core', swap)  2.65 us
  transfers between devices with their start and end apart: 2, of which 2 were waited for; matrix products, arithmetic and copies ran while one was open for 0% of the time, Pallas kernels for 0%

profile of v5, /device:TPU:1, one launch (start us, length us, event | category | flops | bytes accessed | tf_op | source)
XLA Modules:
  0.0 84.3 jit_solution(15411204070518916736)
XLA Ops:
  0.6 1.0 %pad_maximum_fusion.mine = f32[112,960]{1,0:T(8,128)S(1)} fusion(f32[112,576]{1,0:T(8,128)} %bitcast.10, f32[112,384]{1,0:T(8,128)} %bitcast.11), kind=kLoop, calls=%fused_computation | loop fusion | flops 107520 | bytes 860160 | tf_op jit(solution)/shard_map/concatenate | solution.py:351
  1.7 8.8 %collective-permute-start = (f32[112,960]{1,0:T(8,128)S(1)}, f32[112,960]{1,0:T(8,128)S(1)}, u32[]{:S(2)}, u32[]{:S(2)}) collective-permute-start(f32[112,960]{1,0:T(8,128)S(1)} %pad_maximum_fusion.mine), channel_id=1, source_target_pairs={{0,1},{1,0},{2,3},{3,2},{4,5},{5,4},{6,7},{7,6},{8,9},{9,8},{10,11... | collective-permute-start | bytes 1290248 | tf_op jit(solution)/shard_map/ppermute | solution.py:352
  10.5 1.4 %collective-permute-done.other = f32[112,960]{1,0:T(8,128)S(1)} collective-permute-done((f32[112,960]{1,0:T(8,128)S(1)}, f32[112,960]{1,0:T(8,128)S(1)}, u32[]{:S(2)}, u32[]{:S(2)}) %collective-permute-start) | collective-permute-done | bytes 430112 | tf_op jit(solution)/shard_map/ppermute | solution.py:352
  11.9 0.1 chip_sum.1
  12.0 0.0 copy-start
  12.0 0.0 copy-start.1
  12.0 16.0 %all_to_all.15.parts = bf16[4,112,960]{2,1,0:T(8,128)(2,1)S(1)} all-to-all(bf16[4,112,960]{2,1,0:T(8,128)(2,1)S(1)} %chip_sum.1), channel_id=1, replica_groups=mesh['dp'=64,'x'=4,'core'=2] {'x'}, dimensions={0} | all-to-all | bytes 1720320 | tf_op jit(solution)/shard_map/all_to_all | solution.py:354
  28.0 0.0 copy-done
  28.0 0.0 copy-done.1
  28.0 0.9 %momentum_gram.1 = (f32[112,384]{1,0:T(8,128)S(1)}, f32[112,576]{1,0:T(8,128)S(1)}, f32[112,384]{1,0:T(8,128)S(1)}, f32[112,576]{1,0:T(8,128)S(1)}, bf16[1024,128]{1,0:T(8,128)(2,1)S(1)}) custom-call(bf16[4,112,960]{2,1,0:T(8,128)(2,1)S(1)} %all_to_all.15.parts, f32[112,384]{1,0:T(8,128)S(1)} %copy-done.1, f32[112,576]{1,0:T(8,128)S(1)} %copy-done), custom_call_target="tpu_custom_call" | custom-call | tf_op jit(solution)/shard_map/momentum_gram/pallas_call | solution.py:312
  28.9 24.2 %all_to_all.16 = bf16[64,16,128]{2,1,0:T(8,128)(2,1)S(1)} all-to-all(bf16[64,16,128]{2,1,0:T(8,128)(2,1)S(1)} %bitcast.8), channel_id=1, replica_groups=mesh['dp'=64,'x'=4,'core'=2] {'dp'}, dimensions={0} | all-to-all | bytes 524288 | tf_op jit(solution)/shard_map/all_to_all | solution.py:364
  53.1 0.2 scale_gram.1
  53.3 17.3 %all_to_all.17 = bf16[64,16,128]{2,1,0:T(8,128)(2,1)S(1)} all-to-all(bf16[64,16,128]{2,1,0:T(8,128)(2,1)S(1)} %bitcast.9), channel_id=1, replica_groups=mesh['dp'=64,'x'=4,'core'=2] {'dp'}, dimensions={0} | all-to-all | bytes 524288 | tf_op jit(solution)/shard_map/all_to_all | solution.py:370
  70.6 2.8 %router_chain.1.mine = bf16[2176,128]{1,0:T(8,128)(2,1)S(1)} custom-call(bf16[1024,128]{1,0:T(8,128)(2,1)S(1)} %bitcast.6), custom_call_target="tpu_custom_call" | custom-call | tf_op jit(solution)/shard_map/router_chain/pallas_call | solution.py:312
  73.4 2.6 %collective-permute-start.1 = (bf16[2176,128]{1,0:T(8,128)(2,1)S(1)}, bf16[2176,128]{1,0:T(8,128)(2,1)S(1)}, u32[]{:S(2)}, u32[]{:S(2)}) collective-permute-start(bf16[2176,128]{1,0:T(8,128)(2,1)S(1)} %router_chain.1.mine), channel_id=1, source_target_pairs={{0,1},{1,0},{2,3},{3,2},{4,5},{5,4},{6,7},{7,6},{8,9},{9,8},{10,11... | collective-permute-start | bytes 1671176 | tf_op jit(solution)/shard_map/ppermute | solution.py:372
  76.1 1.6 %collective-permute-done.1.other = bf16[2176,128]{1,0:T(8,128)(2,1)S(1)} collective-permute-done((bf16[2176,128]{1,0:T(8,128)(2,1)S(1)}, bf16[2176,128]{1,0:T(8,128)(2,1)S(1)}, u32[]{:S(2)}, u32[]{:S(2)}) %collective-permute-start.1) | collective-permute-done | bytes 557088 | tf_op jit(solution)/shard_map/ppermute | solution.py:372
  77.6 6.6 %chain_apply.1 = (f32[112,384]{1,0:T(8,128)}, f32[112,576]{1,0:T(8,128)}, f32[112,384]{1,0:T(8,128)}, f32[112,576]{1,0:T(8,128)}) custom-call(bf16[2176,128]{1,0:T(8,128)(2,1)S(1)} %router_chain.1.mine, bf16[2176,128]{1,0:T(8,128)(2,1)S(1)} %collective-permute-done.1.other, f32[8,128]{1,0:T(8,128)S(1)} %get-tuple-element.13.magnitude, ...), custom_call_target="tpu_custom_call" | custom-call | tf_op jit(solution)/shard_map/chain_apply/pallas_call | solution.py:334
Async XLA Ops:
  1.7 10.2 %collective-permute-start = (f32[112,960]{1,0:T(8,128)S(1)}, f32[112,960]{1,0:T(8,128)S(1)}, u32[]{:S(2)}, u32[]{:S(2)}) collective-permute-start(f32[112,960]{1,0:T(8,128)S(1)} %pad_maximum_fusion.mine), channel_id=1, source_target_pairs={{0,1},{1,0},{2,3},{3,2},{4,5},{5,4},{6,7},{7,6},{8,9},{9,8},{10,11... | collective-permute-start | bytes 1290248 | tf_op jit(solution)/shard_map/ppermute | solution.py:352
  12.0 16.0 %copy-start = (f32[112,576]{1,0:T(8,128)S(1)}, f32[112,576]{1,0:T(8,128)}, u32[]{:S(2)}) copy-start(f32[112,576]{1,0:T(8,128)} %moment_l.1) | copy-start | bytes 774148
  12.0 16.0 %copy-start.1 = (f32[112,384]{1,0:T(8,128)S(1)}, f32[112,384]{1,0:T(8,128)}, u32[]{:S(2)}) copy-start(f32[112,384]{1,0:T(8,128)} %moment_r.1) | copy-start | bytes 516100
  73.4 4.2 %collective-permute-start.1 = (bf16[2176,128]{1,0:T(8,128)(2,1)S(1)}, bf16[2176,128]{1,0:T(8,128)(2,1)S(1)}, u32[]{:S(2)}, u32[]{:S(2)}) collective-permute-start(bf16[2176,128]{1,0:T(8,128)(2,1)S(1)} %router_chain.1.mine), channel_id=1, source_target_pairs={{0,1},{1,0},{2,3},{3,2},{4,5},{5,4},{6,7},{7,6},{8,9},{9,8},{10,11... | collective-permute-start | bytes 1671176 | tf_op jit(solution)/shard_map/ppermute | solution.py:372

commit v6 on v5

--- a/solution.py
+++ b/solution.py
@@ -178,7 +178,7 @@
     return slab, tile, put, both, unfold
 
 
-def product(left, right, rows, width, epilogue, symmetric=False):
+def strips(left, right, rows, width, epilogue, symmetric=False):
     edge = (rows - 1) // 256 * 256 if symmetric else width
     for start in range(0, edge, 256):
         stop = min(start + 256, edge)
@@ -196,6 +196,20 @@
             ref[edge:rows, edge:width] = value
 
 
+def product(left, right, rows, width, epilogue, symmetric=0):
+    for start in range(0, width, 256):
+        stop = min(start + 256, width)
+        top = start if symmetric else 0
+        acc = dot(left[top:rows, :], right[:, start:stop])
+        for ref, value in epilogue(acc, top, start, stop):
+            ref[top:rows, start:stop] = value
+            if symmetric and stop < width:
+                below = value[stop - top :].astype(F32)
+                if rows < width:
+                    below = jnp.concatenate([below, jnp.zeros((width - rows, 256), F32)], axis=0)
+                ref[start:stop, stop:width] = below.T.astype(BF)
+
+
 def chain(gram, step, mix, fac, tmp, rows, width, symmetric):
     def store(ref):
         return lambda acc, top, start, stop: [(ref, acc.astype(BF))]
@@ -220,10 +234,10 @@
             value = COEF_A * fac[top : top + acc.shape[0], start:stop].astype(F32) + acc
             return [(tmp, value.astype(BF))]
 
-        product(fac, gram, rows, width, store(tmp), symmetric and iteration == 1)
-        product(tmp, fac, rows, width, store(step), symmetric)
-        product(step, step, rows, width, mixing, symmetric)
-        product(mix, fac, rows, width, blend, symmetric)
+        strips(fac, gram, rows, width, store(tmp), symmetric and iteration == 1)
+        strips(tmp, fac, rows, width, store(step), symmetric)
+        strips(step, step, rows, width, mixing, symmetric)
+        strips(mix, fac, rows, width, blend, symmetric)
         fac, tmp = tmp, fac
     return fac
 

time: 84.6 us -> 84.5 us (level)
  no operation moved by 1% of the time
where the time goes in v6:
time: 84.5 us; the launch traced here: 84.2 us
  blocking collectives  57.5 us (68%)
  starting transfers between devices  11.4 us (13%)
  Pallas kernels  10.5 us (12%)
  waiting for transfers between devices  2.98 us (4%)
  other arithmetic  1.04 us (1%)
    all_to_all x1, blocking collectives, local(): pieces = lax.all_to_all(payload.reshape(DP, PIECE, T), 'dp', 0, 0)  24.2 us
    all_to_all x1, blocking collectives, local(): lax.all_to_all(low.reshape(DP, PIECE, T), 'dp', 0, 0).reshape(DP * PIECE, T)  17.3 us
    all_to_all x1, blocking collectives, local(): parts = lax.all_to_all(chip, 'x', 0, 0)  16 us
    ppermute x1, starting transfers between devices, local(): other = lax.ppermute(grads, 'core', swap)  8.79 us
    pallas_call x1, Pallas kernels, chain_call(): pl.pallas_call(update_kernel, out_shape=(shape((ROWS, R), F32), shape((RO...  6.56 us
    pallas_call x4, Pallas kernels, call(): pl.pallas_call(kernel, out_shape=out_shape, in_specs=[VMEM] * len(args),...  3.95 us
    ppermute x1, starting transfers between devices, local(): other = lax.ppermute(mine, 'core', swap)  2.65 us
  transfers between devices with their start and end apart: 2, of which 2 were waited for; matrix products, arithmetic and copies ran while one was open for 0% of the time, Pallas kernels for 0%

profile of v6, /device:TPU:1, one launch (start us, length us, event | category | flops | bytes accessed | tf_op | source)
XLA Modules:
  0.0 84.2 jit_solution(18116427435080404366)
XLA Ops:
  0.6 1.0 %pad_maximum_fusion.mine = f32[112,960]{1,0:T(8,128)S(1)} fusion(f32[112,576]{1,0:T(8,128)} %bitcast.10, f32[112,384]{1,0:T(8,128)} %bitcast.11), kind=kLoop, calls=%fused_computation | loop fusion | flops 107520 | bytes 860160 | tf_op jit(solution)/shard_map/concatenate | solution.py:365
  1.7 8.8 %collective-permute-start = (f32[112,960]{1,0:T(8,128)S(1)}, f32[112,960]{1,0:T(8,128)S(1)}, u32[]{:S(2)}, u32[]{:S(2)}) collective-permute-start(f32[112,960]{1,0:T(8,128)S(1)} %pad_maximum_fusion.mine), channel_id=1, source_target_pairs={{0,1},{1,0},{2,3},{3,2},{4,5},{5,4},{6,7},{7,6},{8,9},{9,8},{10,11... | collective-permute-start | bytes 1290248 | tf_op jit(solution)/shard_map/ppermute | solution.py:366
  10.5 1.4 %collective-permute-done.other = f32[112,960]{1,0:T(8,128)S(1)} collective-permute-done((f32[112,960]{1,0:T(8,128)S(1)}, f32[112,960]{1,0:T(8,128)S(1)}, u32[]{:S(2)}, u32[]{:S(2)}) %collective-permute-start) | collective-permute-done | bytes 430112 | tf_op jit(solution)/shard_map/ppermute | solution.py:366
  11.9 0.1 chip_sum.1
  12.0 0.0 copy-start
  12.0 0.0 copy-start.1
  12.0 16.0 %all_to_all.15.parts = bf16[4,112,960]{2,1,0:T(8,128)(2,1)S(1)} all-to-all(bf16[4,112,960]{2,1,0:T(8,128)(2,1)S(1)} %chip_sum.1), channel_id=1, replica_groups=mesh['dp'=64,'x'=4,'core'=2] {'x'}, dimensions={0} | all-to-all | bytes 1720320 | tf_op jit(solution)/shard_map/all_to_all | solution.py:368
  28.0 0.0 copy-done
  28.0 0.0 copy-done.1
  28.0 0.9 %momentum_gram.1 = (f32[112,384]{1,0:T(8,128)S(1)}, f32[112,576]{1,0:T(8,128)S(1)}, f32[112,384]{1,0:T(8,128)S(1)}, f32[112,576]{1,0:T(8,128)S(1)}, bf16[1024,128]{1,0:T(8,128)(2,1)S(1)}) custom-call(bf16[4,112,960]{2,1,0:T(8,128)(2,1)S(1)} %all_to_all.15.parts, f32[112,384]{1,0:T(8,128)S(1)} %copy-done.1, f32[112,576]{1,0:T(8,128)S(1)} %copy-done), custom_call_target="tpu_custom_call" | custom-call | tf_op jit(solution)/shard_map/momentum_gram/pallas_call | solution.py:326
  28.9 24.2 %all_to_all.16 = bf16[64,16,128]{2,1,0:T(8,128)(2,1)S(1)} all-to-all(bf16[64,16,128]{2,1,0:T(8,128)(2,1)S(1)} %bitcast.8), channel_id=1, replica_groups=mesh['dp'=64,'x'=4,'core'=2] {'dp'}, dimensions={0} | all-to-all | bytes 524288 | tf_op jit(solution)/shard_map/all_to_all | solution.py:378
  53.1 0.2 scale_gram.1
  53.3 17.3 %all_to_all.17 = bf16[64,16,128]{2,1,0:T(8,128)(2,1)S(1)} all-to-all(bf16[64,16,128]{2,1,0:T(8,128)(2,1)S(1)} %bitcast.9), channel_id=1, replica_groups=mesh['dp'=64,'x'=4,'core'=2] {'dp'}, dimensions={0} | all-to-all | bytes 524288 | tf_op jit(solution)/shard_map/all_to_all | solution.py:384
  70.6 2.8 %router_chain.1.mine = bf16[2176,128]{1,0:T(8,128)(2,1)S(1)} custom-call(bf16[1024,128]{1,0:T(8,128)(2,1)S(1)} %bitcast.6), custom_call_target="tpu_custom_call" | custom-call | tf_op jit(solution)/shard_map/router_chain/pallas_call | solution.py:326
  73.4 2.6 %collective-permute-start.1 = (bf16[2176,128]{1,0:T(8,128)(2,1)S(1)}, bf16[2176,128]{1,0:T(8,128)(2,1)S(1)}, u32[]{:S(2)}, u32[]{:S(2)}) collective-permute-start(bf16[2176,128]{1,0:T(8,128)(2,1)S(1)} %router_chain.1.mine), channel_id=1, source_target_pairs={{0,1},{1,0},{2,3},{3,2},{4,5},{5,4},{6,7},{7,6},{8,9},{9,8},{10,11... | collective-permute-start | bytes 1671176 | tf_op jit(solution)/shard_map/ppermute | solution.py:386
  76.1 1.6 %collective-permute-done.1.other = bf16[2176,128]{1,0:T(8,128)(2,1)S(1)} collective-permute-done((bf16[2176,128]{1,0:T(8,128)(2,1)S(1)}, bf16[2176,128]{1,0:T(8,128)(2,1)S(1)}, u32[]{:S(2)}, u32[]{:S(2)}) %collective-permute-start.1) | collective-permute-done | bytes 557088 | tf_op jit(solution)/shard_map/ppermute | solution.py:386
  77.6 6.6 %chain_apply.1 = (f32[112,384]{1,0:T(8,128)}, f32[112,576]{1,0:T(8,128)}, f32[112,384]{1,0:T(8,128)}, f32[112,576]{1,0:T(8,128)}) custom-call(bf16[2176,128]{1,0:T(8,128)(2,1)S(1)} %router_chain.1.mine, bf16[2176,128]{1,0:T(8,128)(2,1)S(1)} %collective-permute-done.1.other, f32[8,128]{1,0:T(8,128)S(1)} %get-tuple-element.13.magnitude, ...), custom_call_target="tpu_custom_call" | custom-call | tf_op jit(solution)/shard_map/chain_apply/pallas_call | solution.py:348
Async XLA Ops:
  1.7 10.2 %collective-permute-start = (f32[112,960]{1,0:T(8,128)S(1)}, f32[112,960]{1,0:T(8,128)S(1)}, u32[]{:S(2)}, u32[]{:S(2)}) collective-permute-start(f32[112,960]{1,0:T(8,128)S(1)} %pad_maximum_fusion.mine), channel_id=1, source_target_pairs={{0,1},{1,0},{2,3},{3,2},{4,5},{5,4},{6,7},{7,6},{8,9},{9,8},{10,11... | collective-permute-start | bytes 1290248 | tf_op jit(solution)/shard_map/ppermute | solution.py:366
  12.0 16.0 %copy-start = (f32[112,576]{1,0:T(8,128)S(1)}, f32[112,576]{1,0:T(8,128)}, u32[]{:S(2)}) copy-start(f32[112,576]{1,0:T(8,128)} %moment_l.1) | copy-start | bytes 774148
  12.0 16.0 %copy-start.1 = (f32[112,384]{1,0:T(8,128)S(1)}, f32[112,384]{1,0:T(8,128)}, u32[]{:S(2)}) copy-start(f32[112,384]{1,0:T(8,128)} %moment_r.1) | copy-start | bytes 516100
  73.4 4.2 %collective-permute-start.1 = (bf16[2176,128]{1,0:T(8,128)(2,1)S(1)}, bf16[2176,128]{1,0:T(8,128)(2,1)S(1)}, u32[]{:S(2)}, u32[]{:S(2)}) collective-permute-start(bf16[2176,128]{1,0:T(8,128)(2,1)S(1)} %router_chain.1.mine), channel_id=1, source_target_pairs={{0,1},{1,0},{2,3},{3,2},{4,5},{5,4},{6,7},{7,6},{8,9},{9,8},{10,11... | collective-permute-start | bytes 1671176 | tf_op jit(solution)/shard_map/ppermute | solution.py:386

commit v7 on v6

--- a/solution.py
+++ b/solution.py
@@ -41,9 +41,7 @@
 
 
 def chip_sum_kernel(mine, other, out):
-    total = (mine[...] + other[...]).astype(BF)
-    for copy in range(4):
-        out[copy] = total
+    out[...] = (mine[...] + other[...]).astype(BF)
 
 
 def split3(value):
@@ -147,13 +145,17 @@
     magnitude[...] = jnp.where(iota((8, T), 0) == 0, router, latent)
 
 
-def unpacker(halves):
+def unpacker(half, early=None):
     row, lane = iota((T, T), 0), iota((T, T), 1)
     lane1 = iota((1, T), 1)
-    extra = halves[0, pl.ds(SLABS, 8, stride=PIECE), :]
+    extra = half[pl.ds(SLABS, 8, stride=PIECE), :]
 
     def slab(g):
-        return halves[g // SLABS, pl.ds(g % SLABS, DP, stride=PIECE), :]
+        if early is None:
+            return half[pl.ds(g, DP, stride=PIECE), :]
+        if g < SLABS:
+            return early[DP * (g - 9) : DP * (g - 8), :]
+        return half[pl.ds(g - SLABS, DP, stride=PIECE), :]
 
     def tile(t):
         return jnp.concatenate([slab(2 * t), slab(2 * t + 1)], axis=0)
@@ -243,11 +245,13 @@
 
 
 def router_kernel(mine, out, half, gram, step, mix, fac, tmp):
-    out[: DP * PIECE, :] = mine[...]
+    @pl.when(lax.axis_index("core") == 0)
+    def _():
+        out[: DP * PIECE, :] = mine[...]
 
     @pl.when(lax.axis_index("core") == 1)
     def _():
-        half[0] = mine[...].astype(F32)
+        half[...] = mine[...].astype(F32)
         slab, tile, put, both, unfold = unpacker(half)
         both(gram, 0, 1, 0)
         both(gram, 0, 2, 1)
@@ -258,13 +262,14 @@
         put(gram, 2, 2, jnp.where(upper, last, last.T))
         factor = chain(gram, step, mix, fac, tmp, R, R, False)
         for j in range(R // T):
-            first = DP * PIECE + R * j
-            out[first : first + R, :] = factor[:, T * j : T * (j + 1)]
+            out[R * j : R * (j + 1), :] = factor[:, T * j : T * (j + 1)]
+        for k in range(6):
+            out[R * R // T + DP * k : R * R // T + DP * (k + 1), :] = slab(9 + k).astype(BF)
 
 
 def update_kernel(
-    mine, other, magnitude, nest_r, nest_l, fresh_r, fresh_l, new_r, new_l, out_r, out_l,
-    halves, gram, step, mix, fac, tmp, fac_r, value_r, value_l, sems,
+    mine, sent, other, magnitude, nest_r, nest_l, fresh_r, fresh_l, new_r, new_l, out_r, out_l,
+    halves, early, gram, step, mix, fac, tmp, fac_r, value_r, value_l, sems,
 ):
     copies = []
 
@@ -276,10 +281,10 @@
     write(fresh_l, new_l)
 
     first = lax.axis_index("core") == 1
-    a, b = mine[: DP * PIECE, :].astype(F32), other[: DP * PIECE, :].astype(F32)
-    halves[0] = jnp.where(first, a, b)
-    halves[1] = jnp.where(first, b, a)
-    slab, tile, put, both, unfold = unpacker(halves)
+    halves[...] = jnp.where(first, other[: DP * PIECE, :], mine[...]).astype(F32)
+    base = R * R // T
+    early[...] = jnp.where(first, sent[base:, :], other[base:, :]).astype(F32)
+    slab, tile, put, both, unfold = unpacker(halves, early)
     gram[L:, :] = jnp.zeros((LP - L, LP), BF)
     gram[512:L, 512:] = jnp.where(iota((64, T), 1) < 64, slab(9), 0.0).astype(BF)
     both(gram, 0, 1, 5)
@@ -313,8 +318,8 @@
             write(value.at[:, start:stop], out.at[:, start:stop])
 
     for j in range(R // T):
-        rows = slice(DP * PIECE + R * j, DP * PIECE + R * (j + 1))
-        fac_r[:, T * j : T * (j + 1)] = jnp.where(first, mine[rows, :], other[rows, :])
+        rows = slice(R * j, R * (j + 1))
+        fac_r[:, T * j : T * (j + 1)] = jnp.where(first, sent[rows, :], other[rows, :])
     apply(nest_r, magnitude[0:1, 0:1], fac_r, R, R, value_r, out_r)
     factor = chain(gram, step, mix, fac, tmp, L, LP, True)
     apply(nest_l, magnitude[1:2, 0:1], factor, L, LP, value_l, out_l)
@@ -337,26 +342,26 @@
 def router_call(mine):
     return call(
         router_kernel,
-        jax.ShapeDtypeStruct((DP * PIECE + R * R // T, T), BF),
-        [pltpu.VMEM((1, DP * PIECE, T), F32)] + [pltpu.VMEM((R, R), BF)] * 5,
+        jax.ShapeDtypeStruct((R * R // T + DP * 6, T), BF),
+        [pltpu.VMEM((DP * PIECE, T), F32)] + [pltpu.VMEM((R, R), BF)] * 5,
         "router_chain", mine,
     )
 
 
-def chain_call(mine, other, magnitude, nest_r, nest_l, fresh_r, fresh_l):
+def chain_call(mine, sent, other, magnitude, nest_r, nest_l, fresh_r, fresh_l):
     shape = jax.ShapeDtypeStruct
     return pl.pallas_call(
         update_kernel,
         out_shape=(shape((ROWS, R), F32), shape((ROWS, L), F32)) * 2,
-        in_specs=[VMEM] * 7,
+        in_specs=[VMEM] * 8,
         out_specs=[pl.BlockSpec(memory_space=pl.ANY)] * 4,
-        scratch_shapes=[pltpu.VMEM((2, DP * PIECE, T), F32)]
+        scratch_shapes=[pltpu.VMEM((DP * PIECE, T), F32), pltpu.VMEM((DP * 6, T), F32)]
         + [pltpu.VMEM((LP, LP), BF)] * 5
         + [pltpu.VMEM((R, R), BF), pltpu.VMEM((ROWS, R), F32), pltpu.VMEM((ROWS, L), F32)]
         + [pltpu.SemaphoreType.DMA((7,))],
         compiler_params=PARAMS,
         name="chain_apply",
-    )(mine, other, magnitude, nest_r, nest_l, fresh_r, fresh_l)
+    )(mine, sent, other, magnitude, nest_r, nest_l, fresh_r, fresh_l)
 
 
 def local(router_grads, latent_grads, router_moment, latent_moment):
@@ -364,8 +369,8 @@
     swap = [(0, 1), (1, 0)]
     grads = lax.optimization_barrier(jnp.concatenate([router_grads[0], latent_grads[0]], axis=1))
     other = lax.ppermute(grads, "core", swap)
-    chip = call(chip_sum_kernel, shape((4, ROWS, R + L), BF), [], "chip_sum", grads, other)
-    parts = lax.all_to_all(chip, "x", 0, 0)
+    chip = call(chip_sum_kernel, shape((ROWS, R + L), BF), [], "chip_sum", grads, other)
+    parts = lax.all_gather(chip, "x")
     fresh_r, fresh_l, nest_r, nest_l, payload = call(
         gram_kernel,
         (
@@ -382,9 +387,9 @@
         [], "scale_gram", pieces.reshape(DP * PIECE, T),
     )
     mine = lax.all_to_all(low.reshape(DP, PIECE, T), "dp", 0, 0).reshape(DP * PIECE, T)
-    mine = router_call(mine)
-    other = lax.ppermute(mine, "core", swap)
-    return chain_call(mine, other, magnitude, nest_r, nest_l, fresh_r, fresh_l)
+    sent = router_call(mine)
+    other = lax.ppermute(sent, "core", swap)
+    return chain_call(mine, sent, other, magnitude, nest_r, nest_l, fresh_r, fresh_l)
 
 
 def solution(mesh):

time: 84.5 us -> 79.9 us (0.946)
  blocking collectives: 57.5 us -> 52.3 us
  starting transfers between devices: 11.4 us -> 12.4 us
    all_to_all x1 -> x0, blocking collectives: 16 us -> none  [local(): parts = lax.all_to_all(chip, 'x', 0, 0)]
    all_gather x0 -> x1, blocking collectives: none -> 11.5 us  [local(): parts = lax.all_gather(chip, 'x')]
    ppermute x1, starting transfers between devices: 2.65 us -> 3.63 us  [local(): other = lax.ppermute(sent, 'core', swap)]
    all_to_all x1, blocking collectives: 17.3 us -> 16.4 us  [local(): lax.all_to_all(low.reshape(DP, PIECE, T), 'dp', 0, 0).reshape(DP * PIECE, T)]
where the time goes in v7:
time: 79.9 us; the launch traced here: 79.7 us
  blocking collectives  52.3 us (65%)
  starting transfers between devices  12.4 us (16%)
  Pallas kernels  10.5 us (13%)
  waiting for transfers between devices  2.75 us (3%)
  other arithmetic  1.04 us (1%)
    all_to_all x1, blocking collectives, local(): pieces = lax.all_to_all(payload.reshape(DP, PIECE, T), 'dp', 0, 0)  24.4 us
    all_to_all x1, blocking collectives, local(): lax.all_to_all(low.reshape(DP, PIECE, T), 'dp', 0, 0).reshape(DP * PIECE, T)  16.4 us
    all_gather x1, blocking collectives, local(): parts = lax.all_gather(chip, 'x')  11.5 us
    ppermute x1, starting transfers between devices, local(): other = lax.ppermute(grads, 'core', swap)  8.79 us
    pallas_call x1, Pallas kernels, chain_call(): pl.pallas_call(update_kernel, out_shape=(shape((ROWS, R), F32), shape((RO...  6.52 us
    pallas_call x4, Pallas kernels, call(): pl.pallas_call(kernel, out_shape=out_shape, in_specs=[VMEM] * len(args),...  3.96 us
    ppermute x1, starting transfers between devices, local(): other = lax.ppermute(sent, 'core', swap)  3.63 us
  transfers between devices with their start and end apart: 2, of which 2 were waited for; matrix products, arithmetic and copies ran while one was open for 0% of the time, Pallas kernels for 0%

profile of v7, /device:TPU:1, one launch (start us, length us, event | category | flops | bytes accessed | tf_op | source)
XLA Modules:
  0.0 79.7 jit_solution(4886259024252280534)
XLA Ops:
  0.6 1.0 %pad_maximum_fusion.mine = f32[112,960]{1,0:T(8,128)S(1)} fusion(f32[112,576]{1,0:T(8,128)} %bitcast.13, f32[112,384]{1,0:T(8,128)} %bitcast.14), kind=kLoop, calls=%fused_computation | loop fusion | flops 107520 | bytes 860160 | tf_op jit(solution)/shard_map/concatenate | solution.py:370
  1.7 8.8 %collective-permute-start = (f32[112,960]{1,0:T(8,128)S(1)}, f32[112,960]{1,0:T(8,128)S(1)}, u32[]{:S(2)}, u32[]{:S(2)}) collective-permute-start(f32[112,960]{1,0:T(8,128)S(1)} %pad_maximum_fusion.mine), channel_id=1, source_target_pairs={{0,1},{1,0},{2,3},{3,2},{4,5},{5,4},{6,7},{7,6},{8,9},{9,8},{10,11... | collective-permute-start | bytes 1290248 | tf_op jit(solution)/shard_map/ppermute | solution.py:371
  10.5 1.4 %collective-permute-done.other = f32[112,960]{1,0:T(8,128)S(1)} collective-permute-done((f32[112,960]{1,0:T(8,128)S(1)}, f32[112,960]{1,0:T(8,128)S(1)}, u32[]{:S(2)}, u32[]{:S(2)}) %collective-permute-start) | collective-permute-done | bytes 430112 | tf_op jit(solution)/shard_map/ppermute | solution.py:371
  11.9 0.0 copy-start
  12.0 0.0 copy-start.1
  12.0 11.5 %all-gather = bf16[448,960]{1,0:T(8,128)(2,1)S(1)} all-gather(bf16[112,960]{1,0:T(8,128)(2,1)S(1)} %chip_sum.1), channel_id=2, replica_groups=mesh['dp'=64,'x'=4,'core'=2] {'x'}, dimensions={0}, use_global_device_ids=true | all-gather | bytes 1075200 | tf_op jit(solution)/shard_map/all_gather | solution.py:373
  23.5 0.0 copy-done
  23.5 0.0 copy-done.1
  23.5 0.9 %momentum_gram.1 = (f32[112,384]{1,0:T(8,128)S(1)}, f32[112,576]{1,0:T(8,128)S(1)}, f32[112,384]{1,0:T(8,128)S(1)}, f32[112,576]{1,0:T(8,128)S(1)}, bf16[1024,128]{1,0:T(8,128)(2,1)S(1)}) custom-call(bf16[4,112,960]{2,1,0:T(8,128)(2,1)S(1)} %bitcast.7, f32[112,384]{1,0:T(8,128)S(1)} %copy-done.1, f32[112,576]{1,0:T(8,128)S(1)} %copy-done), custom_call_target="tpu_custom_call" | custom-call | tf_op jit(solution)/shard_map/momentum_gram/pallas_call | solution.py:331
  24.4 24.4 %all_to_all.10 = bf16[64,16,128]{2,1,0:T(8,128)(2,1)S(1)} all-to-all(bf16[64,16,128]{2,1,0:T(8,128)(2,1)S(1)} %bitcast.11), channel_id=1, replica_groups=mesh['dp'=64,'x'=4,'core'=2] {'dp'}, dimensions={0} | all-to-all | bytes 524288 | tf_op jit(solution)/shard_map/all_to_all | solution.py:383
  48.8 0.2 scale_gram.1
  49.0 16.4 %all_to_all.11 = bf16[64,16,128]{2,1,0:T(8,128)(2,1)S(1)} all-to-all(bf16[64,16,128]{2,1,0:T(8,128)(2,1)S(1)} %bitcast.12), channel_id=1, replica_groups=mesh['dp'=64,'x'=4,'core'=2] {'dp'}, dimensions={0} | all-to-all | bytes 524288 | tf_op jit(solution)/shard_map/all_to_all | solution.py:389
  65.3 2.8 %router_chain.1.sent = bf16[1536,128]{1,0:T(8,128)(2,1)S(1)} custom-call(bf16[1024,128]{1,0:T(8,128)(2,1)S(1)} %bitcast.8), custom_call_target="tpu_custom_call" | custom-call | tf_op jit(solution)/shard_map/router_chain/pallas_call | solution.py:331
  68.2 3.6 %collective-permute-start.1 = (bf16[1536,128]{1,0:T(8,128)(2,1)S(1)}, bf16[1536,128]{1,0:T(8,128)(2,1)S(1)}, u32[]{:S(2)}, u32[]{:S(2)}) collective-permute-start(bf16[1536,128]{1,0:T(8,128)(2,1)S(1)} %router_chain.1.sent), channel_id=1, source_target_pairs={{0,1},{1,0},{2,3},{3,2},{4,5},{5,4},{6,7},{7,6},{8,9},{9,8},{10,11... | collective-permute-start | bytes 1179656 | tf_op jit(solution)/shard_map/ppermute | solution.py:391
  71.8 1.3 %collective-permute-done.1.other = bf16[1536,128]{1,0:T(8,128)(2,1)S(1)} collective-permute-done((bf16[1536,128]{1,0:T(8,128)(2,1)S(1)}, bf16[1536,128]{1,0:T(8,128)(2,1)S(1)}, u32[]{:S(2)}, u32[]{:S(2)}) %collective-permute-start.1) | collective-permute-done | bytes 393248 | tf_op jit(solution)/shard_map/ppermute | solution.py:391
  73.2 6.5 %chain_apply.1 = (f32[112,384]{1,0:T(8,128)}, f32[112,576]{1,0:T(8,128)}, f32[112,384]{1,0:T(8,128)}, f32[112,576]{1,0:T(8,128)}) custom-call(bf16[1024,128]{1,0:T(8,128)(2,1)S(1)} %bitcast.9, bf16[1536,128]{1,0:T(8,128)(2,1)S(1)} %router_chain.1.sent, bf16[1536,128]{1,0:T(8,128)(2,1)S(1)} %collective-permute-done.1.other, ...), custom_call_target="tpu_custom_call" | custom-call | tf_op jit(solution)/shard_map/chain_apply/pallas_call | solution.py:353
  (1 shorter events, 0.0 us)
Async XLA Ops:
  1.7 10.2 %collective-permute-start = (f32[112,960]{1,0:T(8,128)S(1)}, f32[112,960]{1,0:T(8,128)S(1)}, u32[]{:S(2)}, u32[]{:S(2)}) collective-permute-start(f32[112,960]{1,0:T(8,128)S(1)} %pad_maximum_fusion.mine), channel_id=1, source_target_pairs={{0,1},{1,0},{2,3},{3,2},{4,5},{5,4},{6,7},{7,6},{8,9},{9,8},{10,11... | collective-permute-start | bytes 1290248 | tf_op jit(solution)/shard_map/ppermute | solution.py:371
  11.9 11.6 %copy-start = (f32[112,576]{1,0:T(8,128)S(1)}, f32[112,576]{1,0:T(8,128)}, u32[]{:S(2)}) copy-start(f32[112,576]{1,0:T(8,128)} %moment_l.1) | copy-start | bytes 774148
  12.0 11.6 %copy-start.1 = (f32[112,384]{1,0:T(8,128)S(1)}, f32[112,384]{1,0:T(8,128)}, u32[]{:S(2)}) copy-start(f32[112,384]{1,0:T(8,128)} %moment_r.1) | copy-start | bytes 516100
  68.2 5.0 %collective-permute-start.1 = (bf16[1536,128]{1,0:T(8,128)(2,1)S(1)}, bf16[1536,128]{1,0:T(8,128)(2,1)S(1)}, u32[]{:S(2)}, u32[]{:S(2)}) collective-permute-start(bf16[1536,128]{1,0:T(8,128)(2,1)S(1)} %router_chain.1.sent), channel_id=1, source_target_pairs={{0,1},{1,0},{2,3},{3,2},{4,5},{5,4},{6,7},{7,6},{8,9},{9,8},{10,11... | collective-permute-start | bytes 1179656 | tf_op jit(solution)/shard_map/ppermute | solution.py:391

commit v8 on v7

--- a/solution.py
+++ b/solution.py
@@ -40,8 +40,8 @@
     return lax.broadcasted_iota(jnp.int32, shape, dim)
 
 
-def chip_sum_kernel(mine, other, out):
-    out[...] = (mine[...] + other[...]).astype(BF)
+def chip_sum_kernel(two, out):
+    out[...] = (two[0] + two[1]).astype(BF)
 
 
 def split3(value):
@@ -268,7 +268,7 @@
 
 
 def update_kernel(
-    mine, sent, other, magnitude, nest_r, nest_l, fresh_r, fresh_l, new_r, new_l, out_r, out_l,
+    two, magnitude, nest_r, nest_l, fresh_r, fresh_l, new_r, new_l, out_r, out_l,
     halves, early, gram, step, mix, fac, tmp, fac_r, value_r, value_l, sems,
 ):
     copies = []
@@ -280,10 +280,8 @@
     write(fresh_r, new_r)
     write(fresh_l, new_l)
 
-    first = lax.axis_index("core") == 1
-    halves[...] = jnp.where(first, other[: DP * PIECE, :], mine[...]).astype(F32)
-    base = R * R // T
-    early[...] = jnp.where(first, sent[base:, :], other[base:, :]).astype(F32)
+    halves[...] = two[0, : DP * PIECE, :].astype(F32)
+    early[...] = two[1, R * R // T :, :].astype(F32)
     slab, tile, put, both, unfold = unpacker(halves, early)
     gram[L:, :] = jnp.zeros((LP - L, LP), BF)
     gram[512:L, 512:] = jnp.where(iota((64, T), 1) < 64, slab(9), 0.0).astype(BF)
@@ -319,7 +317,7 @@
 
     for j in range(R // T):
         rows = slice(R * j, R * (j + 1))
-        fac_r[:, T * j : T * (j + 1)] = jnp.where(first, sent[rows, :], other[rows, :])
+        fac_r[:, T * j : T * (j + 1)] = two[1, rows, :]
     apply(nest_r, magnitude[0:1, 0:1], fac_r, R, R, value_r, out_r)
     factor = chain(gram, step, mix, fac, tmp, L, LP, True)
     apply(nest_l, magnitude[1:2, 0:1], factor, L, LP, value_l, out_l)
@@ -348,12 +346,12 @@
     )
 
 
-def chain_call(mine, sent, other, magnitude, nest_r, nest_l, fresh_r, fresh_l):
+def chain_call(two, magnitude, nest_r, nest_l, fresh_r, fresh_l):
     shape = jax.ShapeDtypeStruct
     return pl.pallas_call(
         update_kernel,
         out_shape=(shape((ROWS, R), F32), shape((ROWS, L), F32)) * 2,
-        in_specs=[VMEM] * 8,
+        in_specs=[VMEM] * 6,
         out_specs=[pl.BlockSpec(memory_space=pl.ANY)] * 4,
         scratch_shapes=[pltpu.VMEM((DP * PIECE, T), F32), pltpu.VMEM((DP * 6, T), F32)]
         + [pltpu.VMEM((LP, LP), BF)] * 5
@@ -361,15 +359,14 @@
         + [pltpu.SemaphoreType.DMA((7,))],
         compiler_params=PARAMS,
         name="chain_apply",
-    )(mine, sent, other, magnitude, nest_r, nest_l, fresh_r, fresh_l)
+    )(two, magnitude, nest_r, nest_l, fresh_r, fresh_l)
 
 
 def local(router_grads, latent_grads, router_moment, latent_moment):
     shape = jax.ShapeDtypeStruct
-    swap = [(0, 1), (1, 0)]
     grads = lax.optimization_barrier(jnp.concatenate([router_grads[0], latent_grads[0]], axis=1))
-    other = lax.ppermute(grads, "core", swap)
-    chip = call(chip_sum_kernel, shape((ROWS, R + L), BF), [], "chip_sum", grads, other)
+    two = lax.all_gather(grads, "core")
+    chip = call(chip_sum_kernel, shape((ROWS, R + L), BF), [], "chip_sum", two)
     parts = lax.all_gather(chip, "x")
     fresh_r, fresh_l, nest_r, nest_l, payload = call(
         gram_kernel,
@@ -388,8 +385,8 @@
     )
     mine = lax.all_to_all(low.reshape(DP, PIECE, T), "dp", 0, 0).reshape(DP * PIECE, T)
     sent = router_call(mine)
-    other = lax.ppermute(sent, "core", swap)
-    return chain_call(mine, sent, other, magnitude, nest_r, nest_l, fresh_r, fresh_l)
+    two = lax.all_gather(sent, "core")
+    return chain_call(two, magnitude, nest_r, nest_l, fresh_r, fresh_l)
 
 
 def solution(mesh):

time: 79.9 us -> 77.3 us (0.967)
  blocking collectives: 52.3 us -> 65 us
  starting transfers between devices: 12.4 us -> 0 us
  waiting for transfers between devices: 2.75 us -> 0 us
    all_gather x0 -> x2, blocking collectives: none -> 12.7 us  [the longest x1 8.97 us: local(): two = lax.all_gather(grads, 'core')]
    ppermute x2 -> x0, starting transfers between devices: 12.4 us -> none  [the longest x1 8.79 us: local(): other = lax.ppermute(grads, 'core', swap)]
    ppermute x2 -> x0, waiting for transfers between devices: 2.75 us -> none  [the longest x1 1.42 us: local(): other = lax.ppermute(grads, 'core', swap)]
  transfers between devices with their start and end apart: 2 -> 0, of which waited for: 2 -> 0; matrix products, arithmetic and copies ran while one was open for 0% -> 0% of each run, Pallas kernels for 0% -> 0%
where the time goes in v8:
time: 77.3 us; the launch traced here: 77.1 us
  blocking collectives  65 us (84%)
  Pallas kernels  10.4 us (13%)
  other arithmetic  1.04 us (1%)
    all_to_all x1, blocking collectives, local(): pieces = lax.all_to_all(payload.reshape(DP, PIECE, T), 'dp', 0, 0)  24.4 us
    all_to_all x1, blocking collectives, local(): lax.all_to_all(low.reshape(DP, PIECE, T), 'dp', 0, 0).reshape(DP * PIECE, T)  16.4 us
    all_gather x1, blocking collectives, local(): parts = lax.all_gather(chip, 'x')  11.5 us
    all_gather x1, blocking collectives, local(): two = lax.all_gather(grads, 'core')  8.97 us
    pallas_call x1, Pallas kernels, chain_call(): pl.pallas_call(update_kernel, out_shape=(shape((ROWS, R), F32), shape((RO...  6.44 us
    pallas_call x4, Pallas kernels, call(): pl.pallas_call(kernel, out_shape=out_shape, in_specs=[VMEM] * len(args),...  3.95 us
    all_gather x1, blocking collectives, local(): two = lax.all_gather(sent, 'core')  3.74 us

profile of v8, /device:TPU:1, one launch (start us, length us, event | category | flops | bytes accessed | tf_op | source)
XLA Modules:
  0.0 77.1 jit_solution(3029234277386203003)
XLA Ops:
  0.6 1.0 %pad_maximum_fusion = f32[112,960]{1,0:T(8,128)S(1)} fusion(f32[112,576]{1,0:T(8,128)} %bitcast.16, f32[112,384]{1,0:T(8,128)} %bitcast.17), kind=kLoop, calls=%fused_computation | loop fusion | flops 107520 | bytes 860160 | tf_op jit(solution)/shard_map/concatenate | solution.py:367
  1.7 9.0 %all-gather = f32[224,960]{1,0:T(8,128)S(1)} all-gather(f32[112,960]{1,0:T(8,128)S(1)} %pad_maximum_fusion), channel_id=2, replica_groups=mesh['dp'=64,'x'=4,'core'=2] {'core'}, dimensions={0}, use_global_device_ids=true | all-gather | bytes 1290240 | tf_op jit(solution)/shard_map/all_gather | solution.py:368
  10.7 0.0 copy-start
  10.7 0.0 copy-start.1
  10.7 11.5 %all-gather.1 = bf16[448,960]{1,0:T(8,128)(2,1)S(1)} all-gather(bf16[112,960]{1,0:T(8,128)(2,1)S(1)} %chip_sum.1), channel_id=3, replica_groups=mesh['dp'=64,'x'=4,'core'=2] {'x'}, dimensions={0}, use_global_device_ids=true | all-gather | bytes 1075200 | tf_op jit(solution)/shard_map/all_gather | solution.py:370
  22.3 0.0 copy-done
  22.3 0.0 copy-done.1
  22.3 0.9 %momentum_gram.1 = (f32[112,384]{1,0:T(8,128)S(1)}, f32[112,576]{1,0:T(8,128)S(1)}, f32[112,384]{1,0:T(8,128)S(1)}, f32[112,576]{1,0:T(8,128)S(1)}, bf16[1024,128]{1,0:T(8,128)(2,1)S(1)}) custom-call(bf16[4,112,960]{2,1,0:T(8,128)(2,1)S(1)} %bitcast.9, f32[112,384]{1,0:T(8,128)S(1)} %copy-done.1, f32[112,576]{1,0:T(8,128)S(1)} %copy-done), custom_call_target="tpu_custom_call" | custom-call | tf_op jit(solution)/shard_map/momentum_gram/pallas_call | solution.py:329
  23.2 24.4 %all_to_all.10 = bf16[64,16,128]{2,1,0:T(8,128)(2,1)S(1)} all-to-all(bf16[64,16,128]{2,1,0:T(8,128)(2,1)S(1)} %bitcast.14), channel_id=1, replica_groups=mesh['dp'=64,'x'=4,'core'=2] {'dp'}, dimensions={0} | all-to-all | bytes 524288 | tf_op jit(solution)/shard_map/all_to_all | solution.py:380
  47.5 0.2 scale_gram.1
  47.7 16.4 %all_to_all.11 = bf16[64,16,128]{2,1,0:T(8,128)(2,1)S(1)} all-to-all(bf16[64,16,128]{2,1,0:T(8,128)(2,1)S(1)} %bitcast.15), channel_id=1, replica_groups=mesh['dp'=64,'x'=4,'core'=2] {'dp'}, dimensions={0} | all-to-all | bytes 524288 | tf_op jit(solution)/shard_map/all_to_all | solution.py:386
  64.1 2.8 %router_chain.1 = bf16[1536,128]{1,0:T(8,128)(2,1)S(1)} custom-call(bf16[1024,128]{1,0:T(8,128)(2,1)S(1)} %bitcast.13), custom_call_target="tpu_custom_call" | custom-call | tf_op jit(solution)/shard_map/router_chain/pallas_call | solution.py:329
  66.9 3.7 %all-gather.2 = bf16[3072,128]{1,0:T(8,128)(2,1)S(1)} all-gather(bf16[1536,128]{1,0:T(8,128)(2,1)S(1)} %router_chain.1), channel_id=4, replica_groups=mesh['dp'=64,'x'=4,'core'=2] {'core'}, dimensions={0}, use_global_device_ids=true | all-gather | bytes 1179648 | tf_op jit(solution)/shard_map/all_gather | solution.py:388
  70.7 6.4 %chain_apply.1 = (f32[112,384]{1,0:T(8,128)}, f32[112,576]{1,0:T(8,128)}, f32[112,384]{1,0:T(8,128)}, f32[112,576]{1,0:T(8,128)}) custom-call(bf16[2,1536,128]{2,1,0:T(8,128)(2,1)S(1)} %bitcast.11, f32[8,128]{1,0:T(8,128)S(1)} %get-tuple-element.13.magnitude, f32[112,384]{1,0:T(8,128)S(1)} %get-tuple-element.14.nest_r, ...), custom_call_target="tpu_custom_call" | custom-call | tf_op jit(solution)/shard_map/chain_apply/pallas_call | solution.py:351
  (1 shorter events, 0.0 us)
Async XLA Ops:
  10.7 11.6 %copy-start = (f32[112,576]{1,0:T(8,128)S(1)}, f32[112,576]{1,0:T(8,128)}, u32[]{:S(2)}) copy-start(f32[112,576]{1,0:T(8,128)} %moment_l.1) | copy-start | bytes 774148
  10.7 11.6 %copy-start.1 = (f32[112,384]{1,0:T(8,128)S(1)}, f32[112,384]{1,0:T(8,128)}, u32[]{:S(2)}) copy-start(f32[112,384]{1,0:T(8,128)} %moment_r.1) | copy-start | bytes 516100

commit v9 on v8

--- a/solution.py
+++ b/solution.py
@@ -18,6 +18,7 @@
 T = 128
 DP = 64
 SLABS = 15
+XROWS = ROWS * (R + L) // T
 PIECE = 16
 
 COEF_A = 3.4445
@@ -41,7 +42,11 @@
 
 
 def chip_sum_kernel(two, out):
-    out[...] = (two[0] + two[1]).astype(BF)
+    for j in range(7):
+        total = two[0, :, T * j : T * (j + 1)] + two[1, :, T * j : T * (j + 1)]
+        out[ROWS * j : ROWS * (j + 1), :] = total.astype(BF)
+    last = two[0, :, 7 * T :] + two[1, :, 7 * T :]
+    out[7 * ROWS :, :] = jnp.concatenate([last[: ROWS // 2], last[ROWS // 2 :]], axis=1).astype(BF)
 
 
 def split3(value):
@@ -53,14 +58,19 @@
 
 def gram_kernel(parts, moment_r, moment_l, fresh_r, fresh_l, nest_r, nest_l, payload, slabs):
     core = lax.axis_index("core")
+    part = [parts[k].astype(F32) for k in range(4)]
+    total = (part[0] + part[1]) + (part[2] + part[3])
+    last = total[7 * ROWS :]
+    last = jnp.concatenate([last[:, :64], last[:, 64:]], axis=0)
+    total = [total[ROWS * j : ROWS * (j + 1)] for j in range(7)]
+    total = jnp.concatenate(total + [last], axis=1)
     squares = []
     grams = []
     for first, width, moment, new, nest in (
         (0, R, moment_r, fresh_r, nest_r),
         (R, L, moment_l, fresh_l, nest_l),
     ):
-        part = [parts[k, :, first : first + width].astype(F32) for k in range(4)]
-        summed = (part[0] + part[1]) + (part[2] + part[3])
+        summed = total[:, first : first + width]
         fresh = BETA * moment[...] + summed
         nesterov = summed + BETA * fresh
         new[...] = fresh
@@ -366,7 +376,7 @@
     shape = jax.ShapeDtypeStruct
     grads = lax.optimization_barrier(jnp.concatenate([router_grads[0], latent_grads[0]], axis=1))
     two = lax.all_gather(grads, "core")
-    chip = call(chip_sum_kernel, shape((ROWS, R + L), BF), [], "chip_sum", two)
+    chip = call(chip_sum_kernel, shape((XROWS, T), BF), [], "chip_sum", two)
     parts = lax.all_gather(chip, "x")
     fresh_r, fresh_l, nest_r, nest_l, payload = call(
         gram_kernel,

time: 77.3 us -> 77.1 us (level)
  no operation moved by 1% of the time
where the time goes in v9:
time: 77.1 us; the launch traced here: 76.9 us
  blocking collectives  64.8 us (84%)
  Pallas kernels  10.4 us (13%)
  other arithmetic  1.04 us (1%)
    all_to_all x1, blocking collectives, local(): pieces = lax.all_to_all(payload.reshape(DP, PIECE, T), 'dp', 0, 0)  24.3 us
    all_to_all x1, blocking collectives, local(): lax.all_to_all(low.reshape(DP, PIECE, T), 'dp', 0, 0).reshape(DP * PIECE, T)  16.4 us
    all_gather x1, blocking collectives, local(): parts = lax.all_gather(chip, 'x')  11.4 us
    all_gather x1, blocking collectives, local(): two = lax.all_gather(grads, 'core')  8.97 us
    pallas_call x1, Pallas kernels, chain_call(): pl.pallas_call(update_kernel, out_shape=(shape((ROWS, R), F32), shape((RO...  6.44 us
    pallas_call x4, Pallas kernels, call(): pl.pallas_call(kernel, out_shape=out_shape, in_specs=[VMEM] * len(args),...  3.97 us
    all_gather x1, blocking collectives, local(): two = lax.all_gather(sent, 'core')  3.74 us

profile of v9, /device:TPU:1, one launch (start us, length us, event | category | flops | bytes accessed | tf_op | source)
XLA Modules:
  0.0 76.9 jit_solution(17680143040098021522)
XLA Ops:
  0.6 1.0 %pad_maximum_fusion = f32[112,960]{1,0:T(8,128)S(1)} fusion(f32[112,576]{1,0:T(8,128)} %bitcast.16, f32[112,384]{1,0:T(8,128)} %bitcast.17), kind=kLoop, calls=%fused_computation | loop fusion | flops 107520 | bytes 860160 | tf_op jit(solution)/shard_map/concatenate | solution.py:377
  1.7 9.0 %all-gather = f32[224,960]{1,0:T(8,128)S(1)} all-gather(f32[112,960]{1,0:T(8,128)S(1)} %pad_maximum_fusion), channel_id=2, replica_groups=mesh['dp'=64,'x'=4,'core'=2] {'core'}, dimensions={0}, use_global_device_ids=true | all-gather | bytes 1290240 | tf_op jit(solution)/shard_map/all_gather | solution.py:378
  10.6 0.1 chip_sum.1
  10.7 0.0 copy-start
  10.7 0.0 copy-start.1
  10.7 11.4 %all-gather.1 = bf16[3360,128]{1,0:T(8,128)(2,1)S(1)} all-gather(bf16[840,128]{1,0:T(8,128)(2,1)S(1)} %chip_sum.1), channel_id=3, replica_groups=mesh['dp'=64,'x'=4,'core'=2] {'x'}, dimensions={0}, use_global_device_ids=true | all-gather | bytes 1075200 | tf_op jit(solution)/shard_map/all_gather | solution.py:380
  22.1 0.0 copy-done
  22.1 0.0 copy-done.1
  22.1 0.9 %momentum_gram.1 = (f32[112,384]{1,0:T(8,128)S(1)}, f32[112,576]{1,0:T(8,128)S(1)}, f32[112,384]{1,0:T(8,128)S(1)}, f32[112,576]{1,0:T(8,128)S(1)}, bf16[1024,128]{1,0:T(8,128)(2,1)S(1)}) custom-call(bf16[4,840,128]{2,1,0:T(8,128)(2,1)S(1)} %bitcast.10, f32[112,384]{1,0:T(8,128)S(1)} %copy-done.1, f32[112,576]{1,0:T(8,128)S(1)} %copy-done), custom_call_target="tpu_custom_call" | custom-call | tf_op jit(solution)/shard_map/momentum_gram/pallas_call | solution.py:339
  23.0 24.3 %all_to_all.10 = bf16[64,16,128]{2,1,0:T(8,128)(2,1)S(1)} all-to-all(bf16[64,16,128]{2,1,0:T(8,128)(2,1)S(1)} %bitcast.14), channel_id=1, replica_groups=mesh['dp'=64,'x'=4,'core'=2] {'dp'}, dimensions={0} | all-to-all | bytes 524288 | tf_op jit(solution)/shard_map/all_to_all | solution.py:390
  47.3 0.2 scale_gram.1
  47.5 16.4 %all_to_all.11 = bf16[64,16,128]{2,1,0:T(8,128)(2,1)S(1)} all-to-all(bf16[64,16,128]{2,1,0:T(8,128)(2,1)S(1)} %bitcast.15), channel_id=1, replica_groups=mesh['dp'=64,'x'=4,'core'=2] {'dp'}, dimensions={0} | all-to-all | bytes 524288 | tf_op jit(solution)/shard_map/all_to_all | solution.py:396
  63.9 2.8 %router_chain.1 = bf16[1536,128]{1,0:T(8,128)(2,1)S(1)} custom-call(bf16[1024,128]{1,0:T(8,128)(2,1)S(1)} %bitcast.13), custom_call_target="tpu_custom_call" | custom-call | tf_op jit(solution)/shard_map/router_chain/pallas_call | solution.py:339
  66.7 3.7 %all-gather.2 = bf16[3072,128]{1,0:T(8,128)(2,1)S(1)} all-gather(bf16[1536,128]{1,0:T(8,128)(2,1)S(1)} %router_chain.1), channel_id=4, replica_groups=mesh['dp'=64,'x'=4,'core'=2] {'core'}, dimensions={0}, use_global_device_ids=true | all-gather | bytes 1179648 | tf_op jit(solution)/shard_map/all_gather | solution.py:398
  70.4 6.4 %chain_apply.1 = (f32[112,384]{1,0:T(8,128)}, f32[112,576]{1,0:T(8,128)}, f32[112,384]{1,0:T(8,128)}, f32[112,576]{1,0:T(8,128)}) custom-call(bf16[2,1536,128]{2,1,0:T(8,128)(2,1)S(1)} %bitcast.11, f32[8,128]{1,0:T(8,128)S(1)} %get-tuple-element.13.magnitude, f32[112,384]{1,0:T(8,128)S(1)} %get-tuple-element.14.nest_r, ...), custom_call_target="tpu_custom_call" | custom-call | tf_op jit(solution)/shard_map/chain_apply/pallas_call | solution.py:361
Async XLA Ops:
  10.7 11.4 %copy-start = (f32[112,576]{1,0:T(8,128)S(1)}, f32[112,576]{1,0:T(8,128)}, u32[]{:S(2)}) copy-start(f32[112,576]{1,0:T(8,128)} %moment_l.1) | copy-start | bytes 774148
  10.7 11.4 %copy-start.1 = (f32[112,384]{1,0:T(8,128)S(1)}, f32[112,384]{1,0:T(8,128)}, u32[]{:S(2)}) copy-start(f32[112,384]{1,0:T(8,128)} %moment_r.1) | copy-start | bytes 516100
